TPU v7x, 32 devices: a whole 2x2x4 slice. The times are simulated.
32 devices in a mesh: ctx: 8 (over z, core), tp: 4 (over y, x).
Axes of the slice: x: 2, y: 2, z: 4, core: 2. Of those that a mesh axis runs over, the one named last changes fastest.
Arguments:
- x_in: bfloat16 [1024, 16384], P('ctx', 'tp'), may hold values from -6 to 6
- z_in: bfloat16 [1024, 16384], P('ctx', 'tp'), may hold values from -6 to 6
- b_in: bfloat16 [1024, 512], P('ctx', 'tp'), may hold values from -6 to 6
- c_in: bfloat16 [1024, 512], P('ctx', 'tp'), may hold values from -6 to 6
- dt_raw: float32 [1024, 256], P('ctx', 'tp'), may hold values from -2 to 2
- dt_bias: float32 [256], P('tp'), may hold values from -5.8 to -4.2
- a_log: float32 [256], P('tp'), may hold values from -2 to 1.1
- d_skip: float32 [256], P('tp'), may hold values from 0.5 to 1.5
- conv_x: float32 [4, 16384], P(None, 'tp'), may hold values from -3 to 3
- conv_b: float32 [4, 512], P(None, 'tp'), may hold values from -3 to 3
- conv_c: float32 [4, 512], P(None, 'tp'), may hold values from -3 to 3
- norm_gain: float32 [16384], P('tp'), may hold values from 0.1 to 1.9
Outputs:
- mixed_out: bfloat16 [16384, 1024], P(('tp', 'ctx'))
All inputs are finite; a program needn't handle non-finite values.
Results may differ from a plain program's by a relative error of at most 0.007.
Values may be sent and summed in bfloat16 or wider, within the bound.
A program may use at most 128 MiB of HBM per device.

v0:
```python
import jax
import jax.numpy as jnp
from jax import lax
from jax.sharding import PartitionSpec as P

SPAN = 128


def shifted(value, axis, steps):
    count = lax.axis_size(axis)
    initial, last = (max(0, -steps), min(count, count - steps))
    return lax.ppermute(value, axis, [(source, source + steps) for source in range(initial, last)])


def prefix(x, axis, combine, identity):
    length, place = (lax.axis_size(axis), lax.axis_index(axis))
    everything = jax.tree.map(
        lambda part, kind: lax.all_gather(part.astype(kind), axis),
        x,
        jax.tree.map(lambda a: jnp.bfloat16 if a.dtype == jnp.float32 else a.dtype, x),
    )
    start = jax.tree.map(
        lambda part, zero: jnp.broadcast_to(jnp.asarray(zero, part.dtype), part.shape), x, identity
    )

    def lap(k, before):
        reached = k < place
        new = combine(
            before, jax.tree.map(lambda part, own: part[k].astype(own.dtype), everything, x)
        )
        return jax.tree.map(lambda a, b: jnp.where(reached, a, b), new, before)

    return lax.fori_loop(0, length, lap, start)


def causal_silu(padded, taps, length):
    rows_f = padded.astype(jnp.float32)
    total = taps[0] * rows_f[0:length]
    for offset in range(1, taps.shape[0]):
        total = total + taps[offset] * rows_f[offset : offset + length]
    return jax.nn.silu(total).astype(jnp.bfloat16)


def combine(earlier, later):
    return (earlier[0] + later[0], jnp.exp(later[0])[:, None, None] * earlier[1] + later[1])


def shards(
    x_in, z_in, b_in, c_in, dt_raw, dt_bias, a_log, d_skip, conv_x, conv_b, conv_c, norm_gain
):
    length, width = x_in.shape
    heads = dt_raw.shape[1]
    head_size = width // heads
    taps = conv_x.shape[0]
    blocks = length // SPAN
    tails = shifted(
        (x_in[length - taps + 1 :], b_in[length - taps + 1 :], c_in[length - taps + 1 :]), "ctx", 1
    )
    x_act = causal_silu(jnp.concatenate([tails[0], x_in], axis=0), conv_x, length)
    b_act = causal_silu(jnp.concatenate([tails[1], b_in], axis=0), conv_b, length)
    c_act = causal_silu(jnp.concatenate([tails[2], c_in], axis=0), conv_c, length)
    delta = jax.nn.softplus(dt_raw + dt_bias)
    rates = -jnp.exp(a_log) * delta
    logs = jnp.cumsum(rates.reshape(blocks, SPAN, heads), axis=1)
    delta_blocks = delta.reshape(blocks, SPAN, heads)
    x_blocks = x_act.reshape(blocks, SPAN, heads, head_size)
    b_blocks = b_act.reshape(blocks, SPAN, -1)
    c_blocks = c_act.reshape(blocks, SPAN, -1)
    lower = jnp.tril(jnp.ones((SPAN, SPAN), dtype=bool))

    def within_block(item):
        x_part, b_part, c_part, log_part, delta_part = item
        scores = jnp.dot(c_part, b_part.T, preferred_element_type=jnp.float32)
        log_rows = log_part.T
        decay = jnp.exp(
            jnp.where(lower[None], log_rows[:, :, None] - log_rows[:, None, :], -jnp.inf)
        )
        weights = (scores[None] * decay * delta_part.T[:, None, :]).astype(jnp.bfloat16)
        return jnp.einsum("hts,shp->thp", weights, x_part, preferred_element_type=jnp.float32)

    inner = lax.map(within_block, (x_blocks, b_blocks, c_blocks, logs, delta_blocks))
    last = logs[:, -1, :]
    scaled = (
        (jnp.exp(last[:, None, :] - logs) * delta_blocks)[..., None] * x_blocks.astype(jnp.float32)
    ).astype(jnp.bfloat16)
    update = jnp.einsum("cshp,csn->chpn", scaled, b_blocks, preferred_element_type=jnp.float32)
    entering = [jnp.zeros(update.shape[1:], jnp.float32)]
    entering.append(jnp.exp(last[0])[:, None, None] * entering[-1] + update[0])
    own_total = (jnp.sum(last, axis=0), entering[blocks])
    identity = (jnp.zeros_like(own_total[0]), jnp.zeros_like(own_total[1]))
    incoming = prefix(own_total, "ctx", combine, identity)
    before = jnp.cumsum(last, axis=0) - last
    state_in = jnp.exp(before)[:, :, None, None] * incoming[1][None] + jnp.stack(entering[:blocks])
    state_low = state_in.astype(jnp.bfloat16)
    outer = jnp.einsum("ctn,chpn->cthp", c_blocks, state_low, preferred_element_type=jnp.float32)
    y_val = (
        inner + jnp.exp(logs)[..., None] * outer + d_skip[:, None] * x_blocks.astype(jnp.float32)
    )
    gated = y_val.reshape(length, width) * jax.nn.silu(z_in.astype(jnp.float32))
    meansq = jnp.mean(gated * gated, axis=-1, keepdims=True)
    normed = (gated * lax.rsqrt(meansq + 1e-05) * norm_gain).astype(jnp.bfloat16)
    return lax.all_to_all(normed.T, "ctx", split_axis=0, concat_axis=1, tiled=True)


def solution(mesh):
    return jax.shard_map(
        shards,
        mesh=mesh,
        in_specs=(
            P("ctx", "tp"),
            P("ctx", "tp"),
            P("ctx", "tp"),
            P("ctx", "tp"),
            P("ctx", "tp"),
            P("tp"),
            P("tp"),
            P("tp"),
            P(None, "tp"),
            P(None, "tp"),
            P(None, "tp"),
            P("tp"),
        ),
        out_specs=P(("tp", "ctx"), None),
        check_vma=False,
    )
```

profile of v0, /device:TPU:0, one launch (start us, length us, event | category | flops | bytes accessed | tf_op | source)
XLA Modules:
  0.0 168.2 jit_solution(10703676053857746631)
XLA Ops:
  6.5 0.9 slice.85
  7.4 2.4 %collective-permute-start = (bf16[3,4096]{1,0:T(4,128)(2,1)S(1)}, bf16[3,4096]{1,0:T(4,128)(2,1)S(1)}, u32[]{:S(2)}, u32[]{:S(2)}) collective-permute-start(bf16[3,4096]{1,0:T(4,128)(2,1)S(1)} %slice.85), channel_id=1, source_target_pairs={{0,4},{4,8},{8,12},{12,16},{16,20},{20,24},{24,28},{1,5},{5,9},{9,... | collective-permute-start | bytes 73736 | tf_op jit(solution)/shard_map/ppermute | solution.py:12
  9.8 0.7 slice.103
  10.5 4.6 %collective-permute-start.2 = (bf16[3,128]{1,0:T(4,128)(2,1)S(1)}, bf16[3,128]{1,0:T(4,128)(2,1)S(1)}, u32[]{:S(2)}, u32[]{:S(2)}) collective-permute-start(bf16[3,128]{1,0:T(4,128)(2,1)S(1)} %slice.103), channel_id=1, source_target_pairs={{0,4},{4,8},{8,12},{12,16},{16,20},{20,24},{24,28},{1,5},{5,9},{9,... | collective-permute-start | bytes 2312 | tf_op jit(solution)/shard_map/ppermute | solution.py:12
  15.1 0.8 copy.34
  15.9 0.7 exponential_negate_fusion
  16.6 0.7 multiply_bitcast_fusion
  17.3 0.2 reduce_window_sum.17
  17.5 0.7 fusion.30
  18.2 1.1 fusion.31
  19.3 0.8 slice_bitcast_fusion.3
  20.1 1.6 copy.33
  21.7 0.1 copy.39
  21.8 0.0 collective-permute-done.2
  21.8 0.1 multiply_convert_fusion.8
  21.9 0.5 copy.32
  22.4 0.8 maximum_convert_fusion
  23.2 4.9 %fusion.9 = (bf16[128,4096]{0,1:T(8,128)(2,1)S(1)}, bf16[128,4096]{0,1:T(8,128)(2,1)}) fusion(f32[128,64]{0,1:T(8,128)S(1)} %copy.39, f32[131,4096]{0,1:T(8,128)S(1)} %maximum_convert_fusion, f32[4096]{0:T(1024)S(1)} %bitcast.94, f32[4096]{0:T(1024)S(1)} %bitcast.95, f32[4096]{0:T(1024)S(1)} %bitcast.93, f32[4096]{0:T(1024)S(1)} %bitcast.92), kind=kLoop, calls=%fused_computation.20 | loop fusion | flops 7864320 | bytes 10584064 | tf_op jit(solution)/shard_map/convert_element_type | solution.py:85
  28.1 1.5 add_convert_fusion
  29.6 0.0 all-gather.4.cloned.1.call-update
  29.6 1.9 %collective-permute-start.1 = (bf16[3,128]{1,0:T(4,128)(2,1)S(1)}, bf16[3,128]{1,0:T(4,128)(2,1)S(1)}, u32[]{:S(2)}, u32[]{:S(2)}) collective-permute-start(bf16[3,128]{1,0:T(4,128)(2,1)S(1)} %slice.94), channel_id=1, source_target_pairs={{0,4},{4,8},{8,12},{12,16},{16,20},{20,24},{24,28},{1,5},{5,9},{9,... | collective-permute-start | bytes 2312 | tf_op jit(solution)/shard_map/ppermute | solution.py:12
  31.6 10.3 %all-gather = bf16[8,1,64]{2,1,0:T(2,128)(2,1)S(1)} all-gather(bf16[1,1,64]{2,1,0:T(2,128)(2,1)S(1)} %slice.211), channel_id=2, replica_groups=mesh['ctx'=8,'tp'=4] {'ctx'}, dimensions={0}, use_global_device_ids=true | all-gather | bytes 1152 | tf_op jit(solution)/shard_map/all_gather | solution.py:18
  41.9 0.1 copy.37
  41.9 0.1 copy.38
  42.0 0.1 copy.35
  42.1 1.6 copy.40
  43.8 0.1 multiply_convert_fusion.9
  43.8 0.1 fusion.32
  44.0 68.1 %all-gather.4.cloned.1.call-done = bf16[512,64,128]{2,1,0:T(8,128)(2,1)} async-done(((bf16[64,64,128]{2,1,0:T(8,128)(2,1)}), bf16[512,64,128]{2,1,0:T(8,128)(2,1)}) %all-gather.4.cloned.1.call-update) | async-done | bytes 8388624 | tf_op jit(solution)/shard_map/all_gather | solution.py:18
  112.0 14.4 %while.18 = (s32[]{:T(128)}, f32[64,64,128]{2,1,0:T(8,128)S(1)}, s32[]{:T(128)}, bf16[8,64]{1,0:T(8,128)(2,1)S(1)}, bf16[8,64,64,128]{3,2,1,0:T(8,128)(2,1)}, /*index=5*/s32[]{:T(128)}, s32[]{:T(128)}) while((s32[]{:T(128)}, f32[64,64,128]{2,1,0:T(8,128)S(1)}, s32[]{:T(128)}, bf16[8,64]{1,0:T(8,128)(2,1)S(1)}, ...), condition=%wide.region_2.3_spmd.clone, body=%wide.region_1.2_spmd.clone.sunk | while | flops 2621508 | bytes 5243625 | solution.py:33
  112.1 1.8 %fusion.39 = f32[64,64,128]{2,1,0:T(8,128)S(1)} fusion(f32[64,64,128]{2,1,0:T(8,128)S(1)} %get-tuple-element.210, bf16[8,64,64,128]{3,2,1,0:T(8,128)(2,1)} %get-tuple-element.220, s32[]{:T(128)} %get-tuple-element.209, f32[64]{0:T(128)S(1)} %exponential_bitcast_fusion.2, pred[]{:T(512)S(6)} %compare.3, pred[]{:T(512)S(6)} %lt.23), kind=kLoop, calls=%fused_computation.1.clone.1 | loop fusion | flops 2621440 | bytes 5243142 | tf_op jit(solution)/shard_map/while/body/eval_jaxpr/jit(_where)/select_n | solution.py:31
  113.9 1.8 %fusion.39 = f32[64,64,128]{2,1,0:T(8,128)S(1)} fusion(f32[64,64,128]{2,1,0:T(8,128)S(1)} %get-tuple-element.210, bf16[8,64,64,128]{3,2,1,0:T(8,128)(2,1)} %get-tuple-element.220, s32[]{:T(128)} %get-tuple-element.209, f32[64]{0:T(128)S(1)} %exponential_bitcast_fusion.2, pred[]{:T(512)S(6)} %compare.3, pred[]{:T(512)S(6)} %lt.23), kind=kLoop, calls=%fused_computation.1.clone.1 | loop fusion | flops 2621440 | bytes 5243142 | tf_op jit(solution)/shard_map/while/body/eval_jaxpr/jit(_where)/select_n | solution.py:31
  115.7 1.8 %fusion.39 = f32[64,64,128]{2,1,0:T(8,128)S(1)} fusion(f32[64,64,128]{2,1,0:T(8,128)S(1)} %get-tuple-element.210, bf16[8,64,64,128]{3,2,1,0:T(8,128)(2,1)} %get-tuple-element.220, s32[]{:T(128)} %get-tuple-element.209, f32[64]{0:T(128)S(1)} %exponential_bitcast_fusion.2, pred[]{:T(512)S(6)} %compare.3, pred[]{:T(512)S(6)} %lt.23), kind=kLoop, calls=%fused_computation.1.clone.1 | loop fusion | flops 2621440 | bytes 5243142 | tf_op jit(solution)/shard_map/while/body/eval_jaxpr/jit(_where)/select_n | solution.py:31
  117.5 1.8 %fusion.39 = f32[64,64,128]{2,1,0:T(8,128)S(1)} fusion(f32[64,64,128]{2,1,0:T(8,128)S(1)} %get-tuple-element.210, bf16[8,64,64,128]{3,2,1,0:T(8,128)(2,1)} %get-tuple-element.220, s32[]{:T(128)} %get-tuple-element.209, f32[64]{0:T(128)S(1)} %exponential_bitcast_fusion.2, pred[]{:T(512)S(6)} %compare.3, pred[]{:T(512)S(6)} %lt.23), kind=kLoop, calls=%fused_computation.1.clone.1 | loop fusion | flops 2621440 | bytes 5243142 | tf_op jit(solution)/shard_map/while/body/eval_jaxpr/jit(_where)/select_n | solution.py:31
  119.3 1.8 %fusion.39 = f32[64,64,128]{2,1,0:T(8,128)S(1)} fusion(f32[64,64,128]{2,1,0:T(8,128)S(1)} %get-tuple-element.210, bf16[8,64,64,128]{3,2,1,0:T(8,128)(2,1)} %get-tuple-element.220, s32[]{:T(128)} %get-tuple-element.209, f32[64]{0:T(128)S(1)} %exponential_bitcast_fusion.2, pred[]{:T(512)S(6)} %compare.3, pred[]{:T(512)S(6)} %lt.23), kind=kLoop, calls=%fused_computation.1.clone.1 | loop fusion | flops 2621440 | bytes 5243142 | tf_op jit(solution)/shard_map/while/body/eval_jaxpr/jit(_where)/select_n | solution.py:31
  121.1 1.8 %fusion.39 = f32[64,64,128]{2,1,0:T(8,128)S(1)} fusion(f32[64,64,128]{2,1,0:T(8,128)S(1)} %get-tuple-element.210, bf16[8,64,64,128]{3,2,1,0:T(8,128)(2,1)} %get-tuple-element.220, s32[]{:T(128)} %get-tuple-element.209, f32[64]{0:T(128)S(1)} %exponential_bitcast_fusion.2, pred[]{:T(512)S(6)} %compare.3, pred[]{:T(512)S(6)} %lt.23), kind=kLoop, calls=%fused_computation.1.clone.1 | loop fusion | flops 2621440 | bytes 5243142 | tf_op jit(solution)/shard_map/while/body/eval_jaxpr/jit(_where)/select_n | solution.py:31
  122.9 1.8 %fusion.39 = f32[64,64,128]{2,1,0:T(8,128)S(1)} fusion(f32[64,64,128]{2,1,0:T(8,128)S(1)} %get-tuple-element.210, bf16[8,64,64,128]{3,2,1,0:T(8,128)(2,1)} %get-tuple-element.220, s32[]{:T(128)} %get-tuple-element.209, f32[64]{0:T(128)S(1)} %exponential_bitcast_fusion.2, pred[]{:T(512)S(6)} %compare.3, pred[]{:T(512)S(6)} %lt.23), kind=kLoop, calls=%fused_computation.1.clone.1 | loop fusion | flops 2621440 | bytes 5243142 | tf_op jit(solution)/shard_map/while/body/eval_jaxpr/jit(_where)/select_n | solution.py:31
  124.7 1.8 %fusion.39 = f32[64,64,128]{2,1,0:T(8,128)S(1)} fusion(f32[64,64,128]{2,1,0:T(8,128)S(1)} %get-tuple-element.210, bf16[8,64,64,128]{3,2,1,0:T(8,128)(2,1)} %get-tuple-element.220, s32[]{:T(128)} %get-tuple-element.209, f32[64]{0:T(128)S(1)} %exponential_bitcast_fusion.2, pred[]{:T(512)S(6)} %compare.3, pred[]{:T(512)S(6)} %lt.23), kind=kLoop, calls=%fused_computation.1.clone.1 | loop fusion | flops 2621440 | bytes 5243142 | tf_op jit(solution)/shard_map/while/body/eval_jaxpr/jit(_where)/select_n | solution.py:31
  126.5 0.0 copy-start
  126.5 0.0 copy-start.5
  126.5 0.5 fusion.17
  127.0 0.7 copy-done
  127.7 1.8 %fusion.10 = f32[128,64,64]{0,2,1:T(8,128)S(1)} fusion(bf16[128,64,64]{0,2,1:T(8,128)(2,1)S(1)} %bitcast.90, f32[128,64,64]{0,2,1:T(8,128)S(1)} %fusion.17, f32[64,128]{1,0:T(8,128)S(1)} %copy.37, f32[64,128]{1,0:T(8,128)S(1)} %copy.35, f32[128,128]{1,0:T(8,128)S(1)} %fusion.32, pred[128,128]{1,0:T(8,128)(4,1)S(1)} %iota_compare_fusion, ...), kind=kOutput, calls=%fused_computation.22 | convolution fusion | flops 142082048 | bytes 5423360 | tf_op jit(solution)/shard_map/while/body/eval_jaxpr/hts,shp->thp/dot_general | solution.py:79
  129.5 0.0 copy-start.3
  129.5 0.7 multiply_reduce_fusion
  130.3 1.0 multiply_convert_fusion.2
  131.2 29.0 %all_to_all.19 = bf16[8,512,128]{2,1,0:T(8,128)(2,1)S(1)} all-to-all(bf16[8,512,128]{2,1,0:T(8,128)(2,1)S(1)} %bitcast.88), channel_id=1, replica_groups=mesh['ctx'=8,'tp'=4] {'ctx'}, dimensions={0} | all-to-all | bytes 2097152 | tf_op jit(solution)/shard_map/all_to_all | solution.py:102
  160.2 1.1 copy_bitcast_fusion
  (30 shorter events, 0.2 us)
Async XLA Ops:
  6.5 15.3 %copy-start.1 = (bf16[128,128]{1,0:T(8,128)(2,1)S(1)}, bf16[128,128]{1,0:T(8,128)(2,1)}, u32[]{:S(2)}) copy-start(bf16[128,128]{1,0:T(8,128)(2,1)} %param.16) | copy-start | bytes 98308
  6.5 105.5 %all-gather.4.cloned.1.call-start = ((), (), s32[]{:S(2)}) async-start(), calls=%async_computation.1 | async-start | bytes 9437184 | tf_op jit(solution)/shard_map/all_gather | solution.py:18
  7.4 14.5 %collective-permute-start = (bf16[3,4096]{1,0:T(4,128)(2,1)S(1)}, bf16[3,4096]{1,0:T(4,128)(2,1)S(1)}, u32[]{:S(2)}, u32[]{:S(2)}) collective-permute-start(bf16[3,4096]{1,0:T(4,128)(2,1)S(1)} %slice.85), channel_id=1, source_target_pairs={{0,4},{4,8},{8,12},{12,16},{16,20},{20,24},{24,28},{1,5},{5,9},{9,... | collective-permute-start | bytes 73736 | tf_op jit(solution)/shard_map/ppermute | solution.py:12
  10.5 11.3 %collective-permute-start.2 = (bf16[3,128]{1,0:T(4,128)(2,1)S(1)}, bf16[3,128]{1,0:T(4,128)(2,1)S(1)}, u32[]{:S(2)}, u32[]{:S(2)}) collective-permute-start(bf16[3,128]{1,0:T(4,128)(2,1)S(1)} %slice.103), channel_id=1, source_target_pairs={{0,4},{4,8},{8,12},{12,16},{16,20},{20,24},{24,28},{1,5},{5,9},{9,... | collective-permute-start | bytes 2312 | tf_op jit(solution)/shard_map/ppermute | solution.py:12
  28.1 1.5 copy-start.2
  28.1 13.8 %copy-start.4 = (f32[4,128]{1,0:T(4,128)S(1)}, f32[4,128]{1,0:T(4,128)}, u32[]{:S(2)}) copy-start(f32[4,128]{1,0:T(4,128)} %param.24) | copy-start | bytes 6148
  29.6 14.2 %collective-permute-start.1 = (bf16[3,128]{1,0:T(4,128)(2,1)S(1)}, bf16[3,128]{1,0:T(4,128)(2,1)S(1)}, u32[]{:S(2)}, u32[]{:S(2)}) collective-permute-start(bf16[3,128]{1,0:T(4,128)(2,1)S(1)} %slice.94), channel_id=1, source_target_pairs={{0,4},{4,8},{8,12},{12,16},{16,20},{20,24},{24,28},{1,5},{5,9},{9,... | collective-permute-start | bytes 2312 | tf_op jit(solution)/shard_map/ppermute | solution.py:12
  126.5 1.2 copy-start
  126.5 1.2 copy-start.5
  129.5 0.8 copy-start.3
Sparse Core Ops, SparseCore 0:
  29.7 82.2 all-gather.3
where the time goes:
time: 169 us; the launch traced here: 168 us
  waiting for transfers between devices  68.1 us (40%)
  blocking collectives  39.3 us (23%)
  other arithmetic  24 us (14%)
  between operations  13.6 us (8%)
  local copies, waits for them, and re-layouts  10.2 us (6%)
  starting transfers between devices  8.87 us (5%)
  matrix products  3.86 us (2%)
    all_gather x1, waiting for transfers between devices, prefix(): lax.all_gather(part.astype(kind), axis)  68.1 us
    all_to_all x1, blocking collectives, shards(): lax.all_to_all(normed.T, 'ctx', split_axis=0, concat_axis=1, tiled=True)  29 us
    select_n x8, other arithmetic, lap(): return jax.tree.map(lambda a, b: jnp.where(reached, a, b), new, before)  14.2 us
    all_gather x1, blocking collectives, prefix(): lax.all_gather(part.astype(kind), axis)  10.3 us
    ppermute x3, starting transfers between devices, shifted(): lax.ppermute(value, axis, [(source, source + steps) for source in range(i...  8.87 us
    convert_element_type x1, other arithmetic, shards(): scaled = ((jnp.exp(last[:, None, :] - logs) * delta_blocks)[..., None] *...  4.86 us
    unnamed x16, local copies, waits for them, and re-layouts  4.84 us
  transfers between devices with their start and end apart: 4, of which 1 were waited for; matrix products, arithmetic and copies ran while one was open for 6% of the time, Pallas kernels for 0%

commit v1 on v0

v1 whole, which is shorter than its diff:
```python
import functools

import jax
import jax.numpy as jnp
from jax import lax
from jax.experimental import pallas as pl
from jax.experimental.pallas import tpu as pltpu
from jax.sharding import PartitionSpec as P

SPAN = 128
LANES = 128
HALO = 16
CHUNKS = 8
EPS = 1e-05
MESH = pl.DeviceIdType.MESH


def conv_silu(pad, taps, count):
    total = taps[0:1] * pad[8 - count + 1 : 8 - count + 1 + SPAN, :]
    for tap in range(1, count):
        start = 8 - count + 1 + tap
        total = total + taps[tap : tap + 1] * pad[start : start + SPAN, :]
    return (total / (1.0 + jnp.exp(-total))).astype(jnp.bfloat16)


def kernel(
    n,
    x_ref,
    z_ref,
    b_ref,
    c_ref,
    dt_ref,
    bias_ref,
    alog_ref,
    skip_ref,
    cx_ref,
    cb_ref,
    cc_ref,
    gain_ref,
    out_ref,
    halo_x,
    halo_b,
    halo_c,
    small,
    pad,
    x_t,
    z_t,
    upd,
    state_in,
    state_out,
    stage,
    recv,
    scale_in,
    scale_out,
    log_rows,
    mix_rows,
    grow_rows,
    last_rows,
    skip_rows,
    cols,
    scores,
    b_act,
    c_act,
    ssq,
    gain_col,
    halo_send,
    halo_recv,
    state_send,
    state_recv,
    out_send,
    out_recv,
    scale_send,
    scale_recv,
):
    width = x_ref.shape[1]
    heads = dt_ref.shape[1]
    head = width // heads
    per_block = LANES // head
    chunk = width // CHUNKS
    blocks = chunk // LANES
    chunk_heads = heads // CHUNKS
    rows = width // n
    parts = chunk // rows
    taps = cx_ref.shape[0]
    me = lax.axis_index("ctx")
    nxt = lax.rem(me + 1, n)

    barrier = pltpu.get_barrier_semaphore()

    def greet(other, carry):
        @pl.when(other != me)
        def _():
            pl.semaphore_signal(barrier, inc=1, device_id={"ctx": other}, device_id_type=MESH)

        return carry

    lax.fori_loop(0, n, greet, 0)

    def halo_copy(index):
        source = (x_ref, b_ref, c_ref)[index]
        target = (halo_x, halo_b, halo_c)[index]
        return pltpu.make_async_remote_copy(
            src_ref=source.at[pl.ds(SPAN - HALO, HALO), :],
            dst_ref=target,
            send_sem=halo_send.at[index],
            recv_sem=halo_recv.at[index],
            device_id={"ctx": nxt},
            device_id_type=MESH,
        )

    def state_copy(k):
        return pltpu.make_async_remote_copy(
            src_ref=state_out.at[k],
            dst_ref=state_in.at[k],
            send_sem=state_send.at[k],
            recv_sem=state_recv.at[k],
            device_id={"ctx": nxt},
            device_id_type=MESH,
        )

    def out_copy(k, part, dest, slot):
        return pltpu.make_async_remote_copy(
            src_ref=stage.at[k, pl.ds(part * rows, rows), :],
            dst_ref=recv.at[slot],
            send_sem=out_send.at[dest],
            recv_sem=out_recv.at[slot],
            device_id={"ctx": dest},
            device_id_type=MESH,
        )

    def scale_copy(dest, slot):
        return pltpu.make_async_remote_copy(
            src_ref=scale_out,
            dst_ref=scale_in.at[slot],
            send_sem=scale_send.at[dest],
            recv_sem=scale_recv.at[slot],
            device_id={"ctx": dest},
            device_id_type=MESH,
        )

    pl.semaphore_wait(barrier, n - 1)

    @pl.when(me < n - 1)
    def _():
        for index in range(3):
            halo_copy(index).start()

    small[...] = jnp.zeros_like(small)
    small[0:SPAN, 0:heads] = dt_ref[...]
    small[SPAN : SPAN + 1, 0:heads] = bias_ref[...]
    small[SPAN + 8 : SPAN + 9, 0:heads] = alog_ref[...]
    small[SPAN + 16 : SPAN + 17, 0:heads] = skip_ref[...]
    raw = small[0:SPAN, :] + small[SPAN : SPAN + 1, :]
    delta = jnp.maximum(raw, 0.0) + jnp.log1p(jnp.exp(-jnp.abs(raw)))
    rate = -jnp.exp(small[SPAN + 8 : SPAN + 9, :]) * delta
    down = lax.broadcasted_iota(jnp.int32, (SPAN, SPAN), 0)
    across = lax.broadcasted_iota(jnp.int32, (SPAN, SPAN), 1)
    lower = jnp.where(across <= down, 1.0, 0.0)
    logs = jnp.dot(
        lower, rate, precision=lax.Precision.HIGHEST, preferred_element_type=jnp.float32
    )
    last = logs[SPAN - 1 : SPAN, :]
    shifted = logs - jnp.log(delta)
    for k in range(CHUNKS):
        cols[k, :, 0:chunk_heads] = shifted[:, k * chunk_heads : (k + 1) * chunk_heads]
    log_rows[...] = logs.T
    grow_rows[...] = jnp.exp(logs).T
    mix_rows[...] = (jnp.exp(last - logs) * delta).T
    last_rows[...] = jnp.broadcast_to(jnp.exp(last), (SPAN, LANES)).T
    skip_rows[...] = jnp.broadcast_to(small[SPAN + 16 : SPAN + 17, :], (SPAN, LANES)).T
    gain_col[...] = jnp.broadcast_to(gain_ref[...], (SPAN, rows)).T
    ssq[...] = jnp.zeros_like(ssq)

    def turn_z(i, carry):
        place = pl.ds(pl.multiple_of(i * LANES, LANES), LANES)
        value = z_ref[:, place].astype(jnp.float32)
        z_t[place, :] = (value / (1.0 + jnp.exp(-value))).T
        return carry

    lax.fori_loop(0, width // LANES, turn_z, 0)

    @pl.when(me > 0)
    def _():
        for index in range(3):
            halo_copy(index).wait_recv()

    @pl.when(me == 0)
    def _():
        halo_x[...] = jnp.zeros_like(halo_x)
        halo_b[...] = jnp.zeros_like(halo_b)
        halo_c[...] = jnp.zeros_like(halo_c)
        state_in[...] = jnp.zeros_like(state_in)

    for source, halo, weights, target in (
        (b_ref, halo_b, cb_ref, b_act),
        (c_ref, halo_c, cc_ref, c_act),
    ):
        pad[0, 0:8, :] = halo[...].astype(jnp.float32)[HALO - 8 :]
        pad[0, 8 : 8 + SPAN, :] = source[...].astype(jnp.float32)
        target[...] = conv_silu(pad.at[0], weights[...], taps)
    overlap = lax.dot_general(
        b_act[...], c_act[...], (((1,), (1,)), ((), ())), preferred_element_type=jnp.float32
    )
    scores[...] = jnp.where(down <= across, overlap, 0.0)

    def head_row(ref, index):
        return jnp.broadcast_to(ref[pl.ds(index, 1), :], (head, LANES))

    def block_rows(ref, k, j):
        first = k * chunk_heads + j * per_block
        return jnp.concatenate([head_row(ref, first + i) for i in range(per_block)], axis=0)

    def updates(k, carry):
        for j in range(blocks):
            place = pl.ds(pl.multiple_of(k * chunk + j * LANES, LANES), LANES)
            pad[j, 0:8, :] = halo_x[:, place].astype(jnp.float32)[HALO - 8 :]
            pad[j, 8 : 8 + SPAN, :] = x_ref[:, place].astype(jnp.float32)
            act = conv_silu(pad.at[j], cx_ref[:, place], taps)
            turned = act.astype(jnp.float32).T
            x_t[place, :] = turned.astype(jnp.bfloat16)
            scaled = (turned * block_rows(mix_rows, k, j)).astype(jnp.bfloat16)
            upd[place, :] = jnp.dot(scaled, b_act[...], preferred_element_type=jnp.float32)

        @pl.when(me == 0)
        def _():
            place = pl.ds(pl.multiple_of(k * chunk, chunk), chunk)
            state_out[k] = upd[place, :].astype(jnp.bfloat16)
            state_copy(k).start()

        return carry

    lax.fori_loop(0, CHUNKS, updates, 0)

    def outputs(k, carry):
        @pl.when(me > 0)
        def _():
            state_copy(k).wait_recv()

        @pl.when((me > 0) & (me < n - 1))
        def _():
            for j in range(blocks):
                place = pl.ds(pl.multiple_of(k * chunk + j * LANES, LANES), LANES)
                entering = state_in[k, j * LANES : (j + 1) * LANES, :].astype(jnp.float32)
                leaving = block_rows(last_rows, k, j) * entering + upd[place, :]
                state_out[k, j * LANES : (j + 1) * LANES, :] = leaving.astype(jnp.bfloat16)
            state_copy(k).start()

        shifts = cols[k]
        squares = ssq[0:1, :]
        for j in range(blocks):
            place = pl.ds(pl.multiple_of(k * chunk + j * LANES, LANES), LANES)
            x_block = x_t[place, :]
            inner = []
            for i in range(per_block):
                which = j * per_block + i
                gap = (
                    log_rows[pl.ds(k * chunk_heads + which, 1), :] - shifts[:, which : which + 1]
                )
                weights = (scores[...] * jnp.exp(gap)).astype(jnp.bfloat16)
                inner.append(
                    jnp.dot(
                        x_block[i * head : (i + 1) * head],
                        weights,
                        preferred_element_type=jnp.float32,
                    )
                )
            outer = lax.dot_general(
                state_in[k, j * LANES : (j + 1) * LANES, :],
                c_act[...],
                (((1,), (1,)), ((), ())),
                preferred_element_type=jnp.float32,
            )
            y_val = (
                jnp.concatenate(inner, axis=0)
                + block_rows(grow_rows, k, j) * outer
                + block_rows(skip_rows, k, j) * x_block.astype(jnp.float32)
            )
            gated = y_val * z_t[place, :]
            squares = squares + jnp.sum(gated * gated, axis=0, keepdims=True)
            stage[k, j * LANES : (j + 1) * LANES, :] = gated.astype(jnp.bfloat16)
        ssq[0:1, :] = squares

        for part in range(parts):
            dest = k * parts + part

            @pl.when(dest != me)
            def _():
                out_copy(k, part, dest, me).start()

            @pl.when(dest == me)
            def _():
                recv[me] = stage[k, part * rows : (part + 1) * rows, :]

        return carry

    lax.fori_loop(0, CHUNKS, outputs, 0)

    scale = jnp.broadcast_to(lax.rsqrt(ssq[0:1, :] / width + EPS), (8, LANES))
    scale_out[...] = scale
    scale_in[me] = scale

    def tell(other, carry):
        @pl.when(other != me)
        def _():
            scale_copy(other, me).start()

        return carry

    lax.fori_loop(0, n, tell, 0)

    def finish(source, carry):
        @pl.when(source != me)
        def _():
            out_copy(0, 0, source, source).wait_recv()
            scale_copy(source, source).wait_recv()

        place = pl.ds(pl.multiple_of(source * SPAN, SPAN), SPAN)
        value = recv[source].astype(jnp.float32) * scale_in[source][0:1, :] * gain_col[...]
        out_ref[:, place] = value.astype(jnp.bfloat16)
        return carry

    lax.fori_loop(0, n, finish, 0)

    @pl.when(me < n - 1)
    def _():
        for index in range(3):
            halo_copy(index).wait_send()

        def drain_state(k, carry):
            state_copy(k).wait_send()
            return carry

        lax.fori_loop(0, CHUNKS, drain_state, 0)

    def drain(other, carry):
        @pl.when(other != me)
        def _():
            out_copy(0, 0, other, me).wait_send()
            scale_copy(other, me).wait_send()

        return carry

    lax.fori_loop(0, n, drain, 0)


def shards(
    x_in, z_in, b_in, c_in, dt_raw, dt_bias, a_log, d_skip, conv_x, conv_b, conv_c, norm_gain
):
    n = lax.axis_size("ctx")
    width = x_in.shape[1]
    state = b_in.shape[1]
    rows = width // n
    chunk = width // CHUNKS
    own_gain = lax.dynamic_slice_in_dim(norm_gain, lax.axis_index("ctx") * rows, rows)
    vmem = pl.BlockSpec(memory_space=pltpu.VMEM)
    f32, bf16 = jnp.float32, jnp.bfloat16
    dma = pltpu.SemaphoreType.DMA
    square = pltpu.VMEM((LANES, LANES), f32)
    return pl.pallas_call(
        functools.partial(kernel, n),
        out_shape=jax.ShapeDtypeStruct((rows, n * SPAN), bf16),
        in_specs=[vmem] * 12,
        out_specs=vmem,
        scratch_shapes=[
            pltpu.VMEM((HALO, width), bf16),
            pltpu.VMEM((HALO, state), bf16),
            pltpu.VMEM((HALO, state), bf16),
            pltpu.VMEM((SPAN + 24, LANES), f32),
            pltpu.VMEM((max(1, chunk // LANES), SPAN + 8, LANES), f32),
            pltpu.VMEM((width, SPAN), bf16),
            pltpu.VMEM((width, SPAN), f32),
            pltpu.VMEM((width, state), f32),
            pltpu.VMEM((CHUNKS, chunk, state), bf16),
            pltpu.VMEM((CHUNKS, chunk, state), bf16),
            pltpu.VMEM((CHUNKS, chunk, SPAN), bf16),
            pltpu.VMEM((n, rows, SPAN), bf16),
            pltpu.VMEM((n, 8, LANES), f32),
            pltpu.VMEM((8, LANES), f32),
            square,
            square,
            square,
            square,
            square,
            pltpu.VMEM((CHUNKS, SPAN, LANES), f32),
            square,
            pltpu.VMEM((SPAN, state), bf16),
            pltpu.VMEM((SPAN, state), bf16),
            pltpu.VMEM((8, LANES), f32),
            pltpu.VMEM((rows, LANES), f32),
            dma((3,)),
            dma((3,)),
            dma((CHUNKS,)),
            dma((CHUNKS,)),
            dma((n,)),
            dma((n,)),
            dma((n,)),
            dma((n,)),
        ],
        compiler_params=pltpu.CompilerParams(
            collective_id=0, has_side_effects=True, vmem_limit_bytes=40 * 1024 * 1024
        ),
        cost_estimate=pl.CostEstimate(
            flops=8 * SPAN * SPAN * width, bytes_accessed=6 * SPAN * width, transcendentals=0
        ),
    )(
        x_in,
        z_in,
        b_in,
        c_in,
        dt_raw,
        dt_bias[None, :],
        a_log[None, :],
        d_skip[None, :],
        conv_x,
        conv_b,
        conv_c,
        own_gain[None, :],
    )


def solution(mesh):
    return jax.shard_map(
        shards,
        mesh=mesh,
        in_specs=(
            P("ctx", "tp"),
            P("ctx", "tp"),
            P("ctx", "tp"),
            P("ctx", "tp"),
            P("ctx", "tp"),
            P("tp"),
            P("tp"),
            P("tp"),
            P(None, "tp"),
            P(None, "tp"),
            P(None, "tp"),
            P("tp"),
        ),
        out_specs=P(("tp", "ctx"), None),
        check_vma=False,
    )
```

time: 169 us -> 75.8 us (0.45)
  Pallas kernels: 0 us -> 69.4 us
  waiting for transfers between devices: 68.1 us -> 0 us
  blocking collectives: 39.3 us -> 0 us
  other arithmetic: 24 us -> 0 us
  between operations: 13.6 us -> 0.1 us
  starting transfers between devices: 8.87 us -> 0 us
  local copies, waits for them, and re-layouts: 10.2 us -> 5.9 us
  matrix products: 3.86 us -> 0 us
    pallas_call x0 -> x1, Pallas kernels: none -> 69.4 us  [shards(): pl.pallas_call(functools.partial(kernel, n), out_shape=jax.ShapeDtypeStru...]
    all_gather x1 -> x0, waiting for transfers between devices: 68.1 us -> none  [prefix(): lax.all_gather(part.astype(kind), axis)]
    all_to_all x1 -> x0, blocking collectives: 29 us -> none  [shards(): lax.all_to_all(normed.T, 'ctx', split_axis=0, concat_axis=1, tiled=True)]
    select_n x8 -> x0, other arithmetic: 14.2 us -> none  [lap(): return jax.tree.map(lambda a, b: jnp.where(reached, a, b), new, before)]
    all_gather x1 -> x0, blocking collectives: 10.3 us -> none  [prefix(): lax.all_gather(part.astype(kind), axis)]
    ppermute x3 -> x0, starting transfers between devices: 8.87 us -> none  [shifted(): lax.ppermute(value, axis, [(source, source + steps) for source in range(i...]
    convert_element_type x7 -> x0, other arithmetic: 6.74 us -> none  [the longest x1 4.86 us: shards(): scaled = ((jnp.exp(last[:, None, :] - logs) * delta_blocks)[..., None] *...]
    dot_general x4 -> x0, matrix products: 3.86 us -> none  [the longest x1 1.76 us: within_block(): jnp.einsum('hts,shp->thp', weights, x_part, preferred_element_type=jnp.fl...]
  transfers between devices with their start and end apart: 4 -> 0, of which waited for: 1 -> 0; matrix products, arithmetic and copies ran while one was open for 6% -> 0% of each run, Pallas kernels for 0% -> 0%
where the time goes in v1:
time: 75.8 us; the launch traced here: 75.5 us
  Pallas kernels  69.4 us (92%)
  local copies, waits for them, and re-layouts  5.9 us (8%)
    pallas_call x1, Pallas kernels, shards(): pl.pallas_call(functools.partial(kernel, n), out_shape=jax.ShapeDtypeStru...  69.4 us
    unnamed x22, local copies, waits for them, and re-layouts  5.11 us

profile of v1, /device:TPU:0, one launch (start us, length us, event | category | flops | bytes accessed | tf_op | source)
XLA Modules:
  0.0 75.5 jit_solution(14463400929831032672)
XLA Ops:
  0.0 0.0 copy-start.2
  0.0 0.8 %dynamic_slice.3 = f32[512]{0:T(512)S(1)} dynamic-slice(f32[4096]{0:T(1024)} %param.23, s32[]{:T(128)S(6)} %select_n.3), dynamic_slice_sizes={512} | dynamic-slice | bytes 4100 | tf_op jit(solution)/shard_map/dynamic_slice | solution.py:354
  0.8 0.0 copy-start.3
  0.8 0.0 copy-start.5
  0.8 0.0 copy-start.6
  0.8 0.0 copy-start.7
  0.8 0.0 copy-start.8
  0.8 0.0 copy-start.9
  0.8 0.9 %copy.13.dt_ref = f32[128,64]{1,0:T(8,128)S(1)} copy(f32[128,64]{0,1:T(8,128)} %param.16) | data formatting | bytes 65536 | tf_op args[4]
  1.7 0.0 copy-done.2
  1.8 0.0 copy-done.3
  1.8 0.0 copy-done.5
  1.8 0.0 copy-done.6
  1.8 0.0 copy-done.7
  1.8 0.0 copy-done.8
  1.8 0.0 copy-done.9
  1.8 0.0 copy-start
  1.8 1.2 %copy-done = bf16[128,4096]{1,0:T(8,128)(2,1)S(1)} copy-done((bf16[128,4096]{1,0:T(8,128)(2,1)S(1)}, bf16[128,4096]{1,0:T(8,128)(2,1)}, u32[]{:S(2)}) %copy-start) | copy-done | bytes 1048600
  3.0 0.0 copy-start.1
  3.0 1.2 %copy-done.1 = bf16[128,4096]{1,0:T(8,128)(2,1)S(1)} copy-done((bf16[128,4096]{1,0:T(8,128)(2,1)S(1)}, bf16[128,4096]{1,0:T(8,128)(2,1)}, u32[]{:S(2)}) %copy-start.1) | copy-done | bytes 1048600
  4.3 0.0 copy-start.4
  4.3 0.8 %copy-done.4 = bf16[128,128]{1,0:T(8,128)(2,1)S(1)} copy-done((bf16[128,128]{1,0:T(8,128)(2,1)S(1)}, bf16[128,128]{1,0:T(8,128)(2,1)}, u32[]{:S(2)}) %copy-start.4) | copy-done | bytes 32792
  5.0 69.4 %shard_map.118 = bf16[512,1024]{1,0:T(8,128)(2,1)S(1)} custom-call(bf16[128,4096]{1,0:T(8,128)(2,1)S(1)} %copy-done, bf16[128,4096]{1,0:T(8,128)(2,1)S(1)} %copy-done.1, bf16[128,128]{1,0:T(8,128)(2,1)S(1)} %copy-done.3, bf16[128,128]{1,0:T(8,128)(2,1)S(1)} %copy-done.4, f32[128,64]{1,0:T(8,128)S(1)} %copy.13.dt_ref, f32[1,64]{1,0:T(1,128)S(1)} %bitcast.5, ...), custom_call_target="tpu_custom_call" | custom-call | flops 536870912 | bytes 3145728 | tf_op jit(solution)/shard_map/pallas_call | solution.py:359
  74.5 1.0 %copy.15 = bf16[512,1024]{1,0:T(8,128)(2,1)} copy(bf16[512,1024]{1,0:T(8,128)(2,1)S(1)} %shard_map.118) | data formatting | bytes 2097152
Async XLA Ops:
  0.0 1.7 %copy-start.2 = (f32[4,4096]{1,0:T(4,128)S(1)}, f32[4,4096]{1,0:T(4,128)}, u32[]{:S(2)}) copy-start(f32[4,4096]{1,0:T(4,128)} %cx_ref.1) | copy-start | bytes 196612
  0.8 1.0 %copy-start.3 = (bf16[128,128]{1,0:T(8,128)(2,1)S(1)}, bf16[128,128]{1,0:T(8,128)(2,1)}, u32[]{:S(2)}) copy-start(bf16[128,128]{1,0:T(8,128)(2,1)} %b_ref.1) | copy-start | bytes 98308
  0.8 1.0 %copy-start.5 = (f32[4,128]{1,0:T(4,128)S(1)}, f32[4,128]{1,0:T(4,128)}, u32[]{:S(2)}) copy-start(f32[4,128]{1,0:T(4,128)} %cb_ref.1) | copy-start | bytes 6148
  0.8 1.0 %copy-start.6 = (f32[4,128]{1,0:T(4,128)S(1)}, f32[4,128]{1,0:T(4,128)}, u32[]{:S(2)}) copy-start(f32[4,128]{1,0:T(4,128)} %cc_ref.1) | copy-start | bytes 6148
  0.8 1.0 %copy-start.7 = (f32[64]{0:T(128)S(1)}, f32[64]{0:T(128)}, u32[]{:S(2)}) copy-start(f32[64]{0:T(128)} %param.17) | copy-start | bytes 772
  0.8 1.0 %copy-start.8 = (f32[64]{0:T(128)S(1)}, f32[64]{0:T(128)}, u32[]{:S(2)}) copy-start(f32[64]{0:T(128)} %param.18) | copy-start | bytes 772
  0.8 1.0 %copy-start.9 = (f32[64]{0:T(128)S(1)}, f32[64]{0:T(128)}, u32[]{:S(2)}) copy-start(f32[64]{0:T(128)} %param.19) | copy-start | bytes 772
  1.8 1.2 %copy-start = (bf16[128,4096]{1,0:T(8,128)(2,1)S(1)}, bf16[128,4096]{1,0:T(8,128)(2,1)}, u32[]{:S(2)}) copy-start(bf16[128,4096]{1,0:T(8,128)(2,1)} %x_ref.1) | copy-start | bytes 3145732
  3.0 1.2 %copy-start.1 = (bf16[128,4096]{1,0:T(8,128)(2,1)S(1)}, bf16[128,4096]{1,0:T(8,128)(2,1)}, u32[]{:S(2)}) copy-start(bf16[128,4096]{1,0:T(8,128)(2,1)} %z_ref.1) | copy-start | bytes 3145732
  4.3 0.8 %copy-start.4 = (bf16[128,128]{1,0:T(8,128)(2,1)S(1)}, bf16[128,128]{1,0:T(8,128)(2,1)}, u32[]{:S(2)}) copy-start(bf16[128,128]{1,0:T(8,128)(2,1)} %c_ref.1) | copy-start | bytes 98308

commit v2 on v1

--- a/solution.py
+++ b/solution.py
@@ -38,6 +38,13 @@
     cc_ref,
     gain_ref,
     out_ref,
+    x_buf,
+    z_buf,
+    b_buf,
+    c_buf,
+    cx_buf,
+    cb_buf,
+    cc_buf,
     halo_x,
     halo_b,
     halo_c,
@@ -45,6 +52,7 @@
     pad,
     x_t,
     z_t,
+    pre,
     upd,
     state_in,
     state_out,
@@ -63,6 +71,7 @@
     c_act,
     ssq,
     gain_col,
+    load,
     halo_send,
     halo_recv,
     state_send,
@@ -73,7 +82,7 @@
     scale_recv,
 ):
     width = x_ref.shape[1]
-    heads = dt_ref.shape[1]
+    heads = dt_ref.shape[0]
     head = width // heads
     per_block = LANES // head
     chunk = width // CHUNKS
@@ -138,6 +147,42 @@
             device_id_type=MESH,
         )
 
+    def loading(index):
+        source = (x_ref, b_ref, c_ref, cx_ref, cb_ref, cc_ref, z_ref)[index]
+        target = (x_buf, b_buf, c_buf, cx_buf, cb_buf, cc_buf, z_buf)[index]
+        return pltpu.make_async_copy(source, target, load.at[index])
+
+    for index in range(7):
+        loading(index).start()
+
+    def down_columns(row, count):
+        return jnp.broadcast_to(row, (SPAN, count)).T
+
+    small[...] = jnp.zeros_like(small)
+    small[SPAN : SPAN + 1, 0:heads] = bias_ref[...]
+    small[SPAN + 8 : SPAN + 9, 0:heads] = alog_ref[...]
+    small[SPAN + 16 : SPAN + 17, 0:heads] = skip_ref[...]
+    small[0:heads, :] = dt_ref[...]
+    raw = small[0:SPAN, :] + down_columns(small[SPAN : SPAN + 1, :], LANES)
+    delta = jnp.maximum(raw, 0.0) + jnp.log1p(jnp.exp(-jnp.abs(raw)))
+    rate = -down_columns(jnp.exp(small[SPAN + 8 : SPAN + 9, :]), LANES) * delta
+    down = lax.broadcasted_iota(jnp.int32, (SPAN, SPAN), 0)
+    across = lax.broadcasted_iota(jnp.int32, (SPAN, SPAN), 1)
+    upper = jnp.where(down <= across, 1.0, 0.0)
+    logs = jnp.dot(
+        rate, upper, precision=lax.Precision.HIGHEST, preferred_element_type=jnp.float32
+    )
+    last = jnp.broadcast_to(logs[:, SPAN - 1 : SPAN], (SPAN, LANES))
+    log_rows[...] = logs
+    grow_rows[...] = jnp.exp(logs)
+    mix_rows[...] = jnp.exp(last - logs) * delta
+    last_rows[...] = jnp.exp(last)
+    skip_rows[...] = down_columns(small[SPAN + 16 : SPAN + 17, :], LANES)
+    shifted = (logs - jnp.log(delta)).T
+    for k in range(CHUNKS):
+        cols[k, :, 0:chunk_heads] = shifted[:, k * chunk_heads : (k + 1) * chunk_heads]
+    ssq[...] = jnp.zeros_like(ssq)
+
     pl.semaphore_wait(barrier, n - 1)
 
     @pl.when(me < n - 1)
@@ -145,39 +190,13 @@
         for index in range(3):
             halo_copy(index).start()
 
-    small[...] = jnp.zeros_like(small)
-    small[0:SPAN, 0:heads] = dt_ref[...]
-    small[SPAN : SPAN + 1, 0:heads] = bias_ref[...]
-    small[SPAN + 8 : SPAN + 9, 0:heads] = alog_ref[...]
-    small[SPAN + 16 : SPAN + 17, 0:heads] = skip_ref[...]
-    raw = small[0:SPAN, :] + small[SPAN : SPAN + 1, :]
-    delta = jnp.maximum(raw, 0.0) + jnp.log1p(jnp.exp(-jnp.abs(raw)))
-    rate = -jnp.exp(small[SPAN + 8 : SPAN + 9, :]) * delta
-    down = lax.broadcasted_iota(jnp.int32, (SPAN, SPAN), 0)
-    across = lax.broadcasted_iota(jnp.int32, (SPAN, SPAN), 1)
-    lower = jnp.where(across <= down, 1.0, 0.0)
-    logs = jnp.dot(
-        lower, rate, precision=lax.Precision.HIGHEST, preferred_element_type=jnp.float32
-    )
-    last = logs[SPAN - 1 : SPAN, :]
-    shifted = logs - jnp.log(delta)
-    for k in range(CHUNKS):
-        cols[k, :, 0:chunk_heads] = shifted[:, k * chunk_heads : (k + 1) * chunk_heads]
-    log_rows[...] = logs.T
-    grow_rows[...] = jnp.exp(logs).T
-    mix_rows[...] = (jnp.exp(last - logs) * delta).T
-    last_rows[...] = jnp.broadcast_to(jnp.exp(last), (SPAN, LANES)).T
-    skip_rows[...] = jnp.broadcast_to(small[SPAN + 16 : SPAN + 17, :], (SPAN, LANES)).T
-    gain_col[...] = jnp.broadcast_to(gain_ref[...], (SPAN, rows)).T
-    ssq[...] = jnp.zeros_like(ssq)
-
-    def turn_z(i, carry):
-        place = pl.ds(pl.multiple_of(i * LANES, LANES), LANES)
-        value = z_ref[:, place].astype(jnp.float32)
-        z_t[place, :] = (value / (1.0 + jnp.exp(-value))).T
-        return carry
-
-    lax.fori_loop(0, width // LANES, turn_z, 0)
+    if rows % LANES == 0:
+        own_gain = gain_ref[:, pl.ds(pl.multiple_of(me * rows, LANES), rows)]
+    else:
+        own_gain = gain_ref[pl.ds(me, 1), :]
+    gain_col[...] = down_columns(own_gain, rows)
+    for index in range(6):
+        loading(index).wait()
 
     @pl.when(me > 0)
     def _():
@@ -191,13 +210,12 @@
         halo_c[...] = jnp.zeros_like(halo_c)
         state_in[...] = jnp.zeros_like(state_in)
 
-    for source, halo, weights, target in (
-        (b_ref, halo_b, cb_ref, b_act),
-        (c_ref, halo_c, cc_ref, c_act),
+    for index, (source, halo, weights, target) in enumerate(
+        ((b_buf, halo_b, cb_buf, b_act), (c_buf, halo_c, cc_buf, c_act))
     ):
-        pad[0, 0:8, :] = halo[...].astype(jnp.float32)[HALO - 8 :]
-        pad[0, 8 : 8 + SPAN, :] = source[...].astype(jnp.float32)
-        target[...] = conv_silu(pad.at[0], weights[...], taps)
+        pad[index, 0:8, :] = halo[...].astype(jnp.float32)[HALO - 8 :]
+        pad[index, 8 : 8 + SPAN, :] = source[...].astype(jnp.float32)
+        target[...] = conv_silu(pad.at[index], weights[...], taps)
     overlap = lax.dot_general(
         b_act[...], c_act[...], (((1,), (1,)), ((), ())), preferred_element_type=jnp.float32
     )
@@ -210,45 +228,48 @@
         first = k * chunk_heads + j * per_block
         return jnp.concatenate([head_row(ref, first + i) for i in range(per_block)], axis=0)
 
+    def block_place(k, j):
+        return pl.ds(pl.multiple_of(k * chunk + j * LANES, LANES), LANES)
+
+    early = me < n // 2
+
+    def forward(k):
+        for j in range(blocks):
+            entering = state_in[k, j * LANES : (j + 1) * LANES, :].astype(jnp.float32)
+            leaving = block_rows(last_rows, k, j) * entering + upd[block_place(k, j), :]
+            state_out[k, j * LANES : (j + 1) * LANES, :] = leaving.astype(jnp.bfloat16)
+        state_copy(k).start()
+
     def updates(k, carry):
         for j in range(blocks):
-            place = pl.ds(pl.multiple_of(k * chunk + j * LANES, LANES), LANES)
+            place = block_place(k, j)
             pad[j, 0:8, :] = halo_x[:, place].astype(jnp.float32)[HALO - 8 :]
-            pad[j, 8 : 8 + SPAN, :] = x_ref[:, place].astype(jnp.float32)
-            act = conv_silu(pad.at[j], cx_ref[:, place], taps)
+            pad[j, 8 : 8 + SPAN, :] = x_buf[:, place].astype(jnp.float32)
+            act = conv_silu(pad.at[j], cx_buf[:, place], taps)
             turned = act.astype(jnp.float32).T
             x_t[place, :] = turned.astype(jnp.bfloat16)
             scaled = (turned * block_rows(mix_rows, k, j)).astype(jnp.bfloat16)
             upd[place, :] = jnp.dot(scaled, b_act[...], preferred_element_type=jnp.float32)
 
-        @pl.when(me == 0)
-        def _():
-            place = pl.ds(pl.multiple_of(k * chunk, chunk), chunk)
-            state_out[k] = upd[place, :].astype(jnp.bfloat16)
-            state_copy(k).start()
+        @pl.when(early)
+        def _():
+            @pl.when(me > 0)
+            def _():
+                state_copy(k).wait_recv()
+
+            forward(k)
 
         return carry
 
     lax.fori_loop(0, CHUNKS, updates, 0)
-
-    def outputs(k, carry):
-        @pl.when(me > 0)
-        def _():
-            state_copy(k).wait_recv()
-
-        @pl.when((me > 0) & (me < n - 1))
-        def _():
-            for j in range(blocks):
-                place = pl.ds(pl.multiple_of(k * chunk + j * LANES, LANES), LANES)
-                entering = state_in[k, j * LANES : (j + 1) * LANES, :].astype(jnp.float32)
-                leaving = block_rows(last_rows, k, j) * entering + upd[place, :]
-                state_out[k, j * LANES : (j + 1) * LANES, :] = leaving.astype(jnp.bfloat16)
-            state_copy(k).start()
-
+    loading(6).wait()
+
+    def within(k):
         shifts = cols[k]
-        squares = ssq[0:1, :]
         for j in range(blocks):
-            place = pl.ds(pl.multiple_of(k * chunk + j * LANES, LANES), LANES)
+            place = block_place(k, j)
+            value = z_buf[:, place].astype(jnp.float32)
+            z_t[place, :] = (value / (1.0 + jnp.exp(-value))).T
             x_block = x_t[place, :]
             inner = []
             for i in range(per_block):
@@ -264,18 +285,43 @@
                         preferred_element_type=jnp.float32,
                     )
                 )
+            pre[place, :] = jnp.concatenate(inner, axis=0) + block_rows(
+                skip_rows, k, j
+            ) * x_block.astype(jnp.float32)
+
+    ahead = jnp.where(early, 0, jnp.minimum(me - n // 2 + 1, CHUNKS))
+
+    def within_ahead(k, carry):
+        within(k)
+        return carry
+
+    lax.fori_loop(0, ahead, within_ahead, 0)
+
+    def outputs(step, carry):
+        k = jnp.where(early, lax.rem(step + CHUNKS // 2, CHUNKS), step)
+
+        @pl.when(step >= ahead)
+        def _():
+            within(k)
+
+        @pl.when(jnp.logical_not(early))
+        def _():
+            state_copy(k).wait_recv()
+
+            @pl.when(me < n - 1)
+            def _():
+                forward(k)
+
+        squares = ssq[0:1, :]
+        for j in range(blocks):
+            place = block_place(k, j)
             outer = lax.dot_general(
                 state_in[k, j * LANES : (j + 1) * LANES, :],
                 c_act[...],
                 (((1,), (1,)), ((), ())),
                 preferred_element_type=jnp.float32,
             )
-            y_val = (
-                jnp.concatenate(inner, axis=0)
-                + block_rows(grow_rows, k, j) * outer
-                + block_rows(skip_rows, k, j) * x_block.astype(jnp.float32)
-            )
-            gated = y_val * z_t[place, :]
+            gated = (pre[place, :] + block_rows(grow_rows, k, j) * outer) * z_t[place, :]
             squares = squares + jnp.sum(gated * gated, axis=0, keepdims=True)
             stage[k, j * LANES : (j + 1) * LANES, :] = gated.astype(jnp.bfloat16)
         ssq[0:1, :] = squares
@@ -351,7 +397,9 @@
     state = b_in.shape[1]
     rows = width // n
     chunk = width // CHUNKS
-    own_gain = lax.dynamic_slice_in_dim(norm_gain, lax.axis_index("ctx") * rows, rows)
+    gain = norm_gain.reshape((1, width) if rows % LANES == 0 else (n, rows))
+    taps = conv_x.shape[0]
+    hbm = pl.BlockSpec(memory_space=pl.ANY)
     vmem = pl.BlockSpec(memory_space=pltpu.VMEM)
     f32, bf16 = jnp.float32, jnp.bfloat16
     dma = pltpu.SemaphoreType.DMA
@@ -359,15 +407,23 @@
     return pl.pallas_call(
         functools.partial(kernel, n),
         out_shape=jax.ShapeDtypeStruct((rows, n * SPAN), bf16),
-        in_specs=[vmem] * 12,
+        in_specs=[hbm] * 4 + [vmem] * 4 + [hbm] * 3 + [vmem],
         out_specs=vmem,
         scratch_shapes=[
+            pltpu.VMEM((SPAN, width), bf16),
+            pltpu.VMEM((SPAN, width), bf16),
+            pltpu.VMEM((SPAN, state), bf16),
+            pltpu.VMEM((SPAN, state), bf16),
+            pltpu.VMEM((taps, width), f32),
+            pltpu.VMEM((taps, state), f32),
+            pltpu.VMEM((taps, state), f32),
             pltpu.VMEM((HALO, width), bf16),
             pltpu.VMEM((HALO, state), bf16),
             pltpu.VMEM((HALO, state), bf16),
             pltpu.VMEM((SPAN + 24, LANES), f32),
-            pltpu.VMEM((max(1, chunk // LANES), SPAN + 8, LANES), f32),
+            pltpu.VMEM((max(2, chunk // LANES), SPAN + 8, LANES), f32),
             pltpu.VMEM((width, SPAN), bf16),
+            pltpu.VMEM((width, SPAN), f32),
             pltpu.VMEM((width, SPAN), f32),
             pltpu.VMEM((width, state), f32),
             pltpu.VMEM((CHUNKS, chunk, state), bf16),
@@ -387,6 +443,7 @@
             pltpu.VMEM((SPAN, state), bf16),
             pltpu.VMEM((8, LANES), f32),
             pltpu.VMEM((rows, LANES), f32),
+            dma((7,)),
             dma((3,)),
             dma((3,)),
             dma((CHUNKS,)),
@@ -397,7 +454,7 @@
             dma((n,)),
         ],
         compiler_params=pltpu.CompilerParams(
-            collective_id=0, has_side_effects=True, vmem_limit_bytes=40 * 1024 * 1024
+            collective_id=0, has_side_effects=True, vmem_limit_bytes=56 * 1024 * 1024
         ),
         cost_estimate=pl.CostEstimate(
             flops=8 * SPAN * SPAN * width, bytes_accessed=6 * SPAN * width, transcendentals=0
@@ -407,14 +464,14 @@
         z_in,
         b_in,
         c_in,
-        dt_raw,
+        dt_raw.T,
         dt_bias[None, :],
         a_log[None, :],
         d_skip[None, :],
         conv_x,
         conv_b,
         conv_c,
-        own_gain[None, :],
+        gain,
     )
 
 

time: 75.8 us -> 62.3 us (0.82)
  Pallas kernels: 69.4 us -> 59.8 us
  local copies, waits for them, and re-layouts: 5.9 us -> 2.26 us
    pallas_call x1, Pallas kernels: 69.4 us -> 59.8 us  [shards(): pl.pallas_call(functools.partial(kernel, n), out_shape=jax.ShapeDtypeStru...]
    unnamed x22 -> x1, local copies, waits for them, and re-layouts: 5.11 us -> 2.26 us
    dynamic_slice x1 -> x0, local copies, waits for them, and re-layouts: 0.79 us -> none  [shards(): lax.dynamic_slice_in_dim(norm_gain, lax.axis_index('ctx') * rows, rows)]
where the time goes in v2:
time: 62.3 us; the launch traced here: 62.1 us
  Pallas kernels  59.8 us (96%)
  local copies, waits for them, and re-layouts  2.26 us (4%)
    pallas_call x1, Pallas kernels, shards(): pl.pallas_call(functools.partial(kernel, n), out_shape=jax.ShapeDtypeStru...  59.8 us
    unnamed x1, local copies, waits for them, and re-layouts  2.26 us

profile of v2, /device:TPU:0, one launch (start us, length us, event | category | flops | bytes accessed | tf_op | source)
XLA Modules:
  0.0 62.1 jit_solution(3627010340198290056)
XLA Ops:
  0.0 59.8 %shard_map.118 = bf16[512,1024]{1,0:T(8,128)(2,1)} custom-call(bf16[128,4096]{1,0:T(8,128)(2,1)} %x_ref.1, bf16[128,4096]{1,0:T(8,128)(2,1)} %z_ref.1, bf16[128,128]{1,0:T(8,128)(2,1)} %b_ref.1, bf16[128,128]{1,0:T(8,128)(2,1)} %c_ref.1, f32[64,128]{1,0:T(8,128)} %bitcast.5, f32[1,64]{1,0:T(1,128)} %bitcast.7, f32[1,64]{1,0:T(1,128)} %bitcast.8, ...), custom_call_target="tpu_custom_call" | custom-call | flops 536870912 | bytes 3145728 | tf_op jit(solution)/shard_map/pallas_call | solution.py:407
  59.8 2.3 %copy.14 = bf16[512,1024]{1,0:T(8,128)(2,1)} copy(bf16[512,1024]{1,0:T(8,128)(2,1)} %shard_map.118) | data formatting | bytes 2097152

commit v3 on v2

--- a/solution.py
+++ b/solution.py
@@ -12,7 +12,13 @@
 HALO = 16
 CHUNKS = 8
 EPS = 1e-05
+LOG2E = 1.4426950408889634
 MESH = pl.DeviceIdType.MESH
+
+
+def silu(value):
+    half = 0.5 * value
+    return half + half * jnp.tanh(half)
 
 
 def conv_silu(pad, taps, count):
@@ -20,7 +26,7 @@
     for tap in range(1, count):
         start = 8 - count + 1 + tap
         total = total + taps[tap : tap + 1] * pad[start : start + SPAN, :]
-    return (total / (1.0 + jnp.exp(-total))).astype(jnp.bfloat16)
+    return silu(total).astype(jnp.bfloat16)
 
 
 def kernel(
@@ -36,8 +42,8 @@
     cx_ref,
     cb_ref,
     cc_ref,
-    gain_ref,
-    out_ref,
+    recv,
+    scale_in,
     x_buf,
     z_buf,
     b_buf,
@@ -57,8 +63,6 @@
     state_in,
     state_out,
     stage,
-    recv,
-    scale_in,
     scale_out,
     log_rows,
     mix_rows,
@@ -70,7 +74,6 @@
     b_act,
     c_act,
     ssq,
-    gain_col,
     load,
     halo_send,
     halo_recv,
@@ -137,6 +140,14 @@
             device_id_type=MESH,
         )
 
+    def own_out(k, part):
+        return pltpu.make_async_copy(
+            stage.at[k, pl.ds(part * rows, rows), :], recv.at[me], out_recv.at[me]
+        )
+
+    def own_scale():
+        return pltpu.make_async_copy(scale_out, scale_in.at[me], scale_recv.at[me])
+
     def scale_copy(dest, slot):
         return pltpu.make_async_remote_copy(
             src_ref=scale_out,
@@ -173,12 +184,12 @@
         rate, upper, precision=lax.Precision.HIGHEST, preferred_element_type=jnp.float32
     )
     last = jnp.broadcast_to(logs[:, SPAN - 1 : SPAN], (SPAN, LANES))
-    log_rows[...] = logs
+    log_rows[...] = logs * LOG2E
     grow_rows[...] = jnp.exp(logs)
     mix_rows[...] = jnp.exp(last - logs) * delta
     last_rows[...] = jnp.exp(last)
     skip_rows[...] = down_columns(small[SPAN + 16 : SPAN + 17, :], LANES)
-    shifted = (logs - jnp.log(delta)).T
+    shifted = ((logs - jnp.log(delta)) * LOG2E).T
     for k in range(CHUNKS):
         cols[k, :, 0:chunk_heads] = shifted[:, k * chunk_heads : (k + 1) * chunk_heads]
     ssq[...] = jnp.zeros_like(ssq)
@@ -190,11 +201,6 @@
         for index in range(3):
             halo_copy(index).start()
 
-    if rows % LANES == 0:
-        own_gain = gain_ref[:, pl.ds(pl.multiple_of(me * rows, LANES), rows)]
-    else:
-        own_gain = gain_ref[pl.ds(me, 1), :]
-    gain_col[...] = down_columns(own_gain, rows)
     for index in range(6):
         loading(index).wait()
 
@@ -246,9 +252,9 @@
             pad[j, 0:8, :] = halo_x[:, place].astype(jnp.float32)[HALO - 8 :]
             pad[j, 8 : 8 + SPAN, :] = x_buf[:, place].astype(jnp.float32)
             act = conv_silu(pad.at[j], cx_buf[:, place], taps)
-            turned = act.astype(jnp.float32).T
-            x_t[place, :] = turned.astype(jnp.bfloat16)
-            scaled = (turned * block_rows(mix_rows, k, j)).astype(jnp.bfloat16)
+            turned = act.T
+            x_t[place, :] = turned
+            scaled = (turned.astype(jnp.float32) * block_rows(mix_rows, k, j)).astype(jnp.bfloat16)
             upd[place, :] = jnp.dot(scaled, b_act[...], preferred_element_type=jnp.float32)
 
         @pl.when(early)
@@ -268,8 +274,7 @@
         shifts = cols[k]
         for j in range(blocks):
             place = block_place(k, j)
-            value = z_buf[:, place].astype(jnp.float32)
-            z_t[place, :] = (value / (1.0 + jnp.exp(-value))).T
+            z_t[place, :] = silu(z_buf[:, place].T.astype(jnp.float32))
             x_block = x_t[place, :]
             inner = []
             for i in range(per_block):
@@ -277,7 +282,7 @@
                 gap = (
                     log_rows[pl.ds(k * chunk_heads + which, 1), :] - shifts[:, which : which + 1]
                 )
-                weights = (scores[...] * jnp.exp(gap)).astype(jnp.bfloat16)
+                weights = (scores[...] * jnp.exp2(gap)).astype(jnp.bfloat16)
                 inner.append(
                     jnp.dot(
                         x_block[i * head : (i + 1) * head],
@@ -289,7 +294,7 @@
                 skip_rows, k, j
             ) * x_block.astype(jnp.float32)
 
-    ahead = jnp.where(early, 0, jnp.minimum(me - n // 2 + 1, CHUNKS))
+    ahead = jnp.where(early, 0, jnp.minimum(2 * (me - n // 2) + 2, CHUNKS))
 
     def within_ahead(k, carry):
         within(k)
@@ -335,7 +340,7 @@
 
             @pl.when(dest == me)
             def _():
-                recv[me] = stage[k, part * rows : (part + 1) * rows, :]
+                own_out(k, part).start()
 
         return carry
 
@@ -343,7 +348,7 @@
 
     scale = jnp.broadcast_to(lax.rsqrt(ssq[0:1, :] / width + EPS), (8, LANES))
     scale_out[...] = scale
-    scale_in[me] = scale
+    own_scale().start()
 
     def tell(other, carry):
         @pl.when(other != me)
@@ -360,9 +365,11 @@
             out_copy(0, 0, source, source).wait_recv()
             scale_copy(source, source).wait_recv()
 
-        place = pl.ds(pl.multiple_of(source * SPAN, SPAN), SPAN)
-        value = recv[source].astype(jnp.float32) * scale_in[source][0:1, :] * gain_col[...]
-        out_ref[:, place] = value.astype(jnp.bfloat16)
+        @pl.when(source == me)
+        def _():
+            own_out(0, 0).wait()
+            own_scale().wait()
+
         return carry
 
     lax.fori_loop(0, n, finish, 0)
@@ -387,6 +394,22 @@
         return carry
 
     lax.fori_loop(0, n, drain, 0)
+
+
+def normalise(gated_ref, scale_ref, gain_ref, out_ref, gain_col):
+    rows = out_ref.shape[0]
+    me = lax.axis_index("ctx")
+
+    @pl.when(pl.program_id(0) == 0)
+    def _():
+        if rows % LANES == 0:
+            own = gain_ref[:, pl.ds(pl.multiple_of(me * rows, LANES), rows)]
+        else:
+            own = gain_ref[pl.ds(me, 1), :]
+        gain_col[...] = jnp.broadcast_to(own, (LANES, rows)).T
+
+    value = gated_ref[0].astype(jnp.float32) * scale_ref[0, 0:1, :] * gain_col[...]
+    out_ref[...] = value.astype(jnp.bfloat16)
 
 
 def shards(
@@ -404,11 +427,14 @@
     f32, bf16 = jnp.float32, jnp.bfloat16
     dma = pltpu.SemaphoreType.DMA
     square = pltpu.VMEM((LANES, LANES), f32)
-    return pl.pallas_call(
+    gated, scales = pl.pallas_call(
         functools.partial(kernel, n),
-        out_shape=jax.ShapeDtypeStruct((rows, n * SPAN), bf16),
-        in_specs=[hbm] * 4 + [vmem] * 4 + [hbm] * 3 + [vmem],
-        out_specs=vmem,
+        out_shape=(
+            jax.ShapeDtypeStruct((n, rows, SPAN), bf16),
+            jax.ShapeDtypeStruct((n, 8, LANES), f32),
+        ),
+        in_specs=[hbm] * 4 + [vmem] * 4 + [hbm] * 3,
+        out_specs=(hbm, hbm),
         scratch_shapes=[
             pltpu.VMEM((SPAN, width), bf16),
             pltpu.VMEM((SPAN, width), bf16),
@@ -429,8 +455,6 @@
             pltpu.VMEM((CHUNKS, chunk, state), bf16),
             pltpu.VMEM((CHUNKS, chunk, state), bf16),
             pltpu.VMEM((CHUNKS, chunk, SPAN), bf16),
-            pltpu.VMEM((n, rows, SPAN), bf16),
-            pltpu.VMEM((n, 8, LANES), f32),
             pltpu.VMEM((8, LANES), f32),
             square,
             square,
@@ -442,7 +466,6 @@
             pltpu.VMEM((SPAN, state), bf16),
             pltpu.VMEM((SPAN, state), bf16),
             pltpu.VMEM((8, LANES), f32),
-            pltpu.VMEM((rows, LANES), f32),
             dma((7,)),
             dma((3,)),
             dma((3,)),
@@ -471,8 +494,20 @@
         conv_x,
         conv_b,
         conv_c,
-        gain,
     )
+    return pl.pallas_call(
+        normalise,
+        grid=(n,),
+        out_shape=jax.ShapeDtypeStruct((rows, n * SPAN), bf16),
+        in_specs=[
+            pl.BlockSpec((1, rows, SPAN), lambda i: (i, 0, 0)),
+            pl.BlockSpec((1, 8, LANES), lambda i: (i, 0, 0)),
+            pl.BlockSpec(gain.shape, lambda i: (0, 0)),
+        ],
+        out_specs=pl.BlockSpec((rows, SPAN), lambda i: (0, i)),
+        scratch_shapes=[pltpu.VMEM((rows, LANES), f32)],
+        compiler_params=pltpu.CompilerParams(vmem_limit_bytes=56 * 1024 * 1024),
+    )(gated, scales, gain)
 
 
 def solution(mesh):

time: 62.3 us -> 65.1 us (1.045)
  Pallas kernels: 59.8 us -> 64.8 us
  local copies, waits for them, and re-layouts: 2.26 us -> 0 us
    pallas_call x1 -> x2, Pallas kernels: 59.8 us -> 64.8 us  [the longest x1 59.4 us: shards(): pl.pallas_call(functools.partial(kernel, n), out_shape=(jax.ShapeDtypeStr...]
    unnamed x1 -> x0, local copies, waits for them, and re-layouts: 2.26 us -> none
where the time goes in v3:
time: 65.1 us; the launch traced here: 64.8 us
  Pallas kernels  64.8 us (100%)
    pallas_call x1, Pallas kernels, shards(): pl.pallas_call(functools.partial(kernel, n), out_shape=(jax.ShapeDtypeStr...  59.4 us
    pallas_call x1, Pallas kernels, shards(): pl.pallas_call(normalise, grid=(n,), out_shape=jax.ShapeDtypeStruct((rows...  5.42 us

profile of v3, /device:TPU:0, one launch (start us, length us, event | category | flops | bytes accessed | tf_op | source)
XLA Modules:
  0.0 64.8 jit_solution(1294302001798215928)
XLA Ops:
  0.0 59.4 %shard_map.118 = (bf16[8,512,128]{2,1,0:T(8,128)(2,1)}, f32[8,8,128]{2,1,0:T(8,128)}) custom-call(bf16[128,4096]{1,0:T(8,128)(2,1)} %x_ref.1, bf16[128,4096]{1,0:T(8,128)(2,1)} %z_ref.1, bf16[128,128]{1,0:T(8,128)(2,1)} %b_ref.1, bf16[128,128]{1,0:T(8,128)(2,1)} %c_ref.1, f32[64,128]{1,0:T(8,128)} %bitcast.5, f32[1,64]{1,0:T(1,128)} %bitcast.7, ...), custom_call_target="tpu_custom_call" | custom-call | flops 536870912 | bytes 3145728 | tf_op jit(solution)/shard_map/pallas_call | solution.py:430
  59.4 5.4 %shard_map.119 = bf16[512,1024]{1,0:T(8,128)(2,1)} custom-call(bf16[8,512,128]{2,1,0:T(8,128)(2,1)} %get-tuple-element.7.gated_ref, f32[8,8,128]{2,1,0:T(8,128)} %get-tuple-element.8.scale_ref, f32[1,4096]{1,0:T(1,128)} %bitcast.6), custom_call_target="tpu_custom_call" | custom-call | tf_op jit(solution)/shard_map/pallas_call | solution.py:498

commit v4 on v2

--- a/solution.py
+++ b/solution.py
@@ -12,7 +12,13 @@
 HALO = 16
 CHUNKS = 8
 EPS = 1e-05
+LOG2E = 1.4426950408889634
 MESH = pl.DeviceIdType.MESH
+
+
+def silu(value):
+    half = 0.5 * value
+    return half + half * jnp.tanh(half)
 
 
 def conv_silu(pad, taps, count):
@@ -20,7 +26,7 @@
     for tap in range(1, count):
         start = 8 - count + 1 + tap
         total = total + taps[tap : tap + 1] * pad[start : start + SPAN, :]
-    return (total / (1.0 + jnp.exp(-total))).astype(jnp.bfloat16)
+    return silu(total).astype(jnp.bfloat16)
 
 
 def kernel(
@@ -173,12 +179,12 @@
         rate, upper, precision=lax.Precision.HIGHEST, preferred_element_type=jnp.float32
     )
     last = jnp.broadcast_to(logs[:, SPAN - 1 : SPAN], (SPAN, LANES))
-    log_rows[...] = logs
+    log_rows[...] = logs * LOG2E
     grow_rows[...] = jnp.exp(logs)
     mix_rows[...] = jnp.exp(last - logs) * delta
     last_rows[...] = jnp.exp(last)
     skip_rows[...] = down_columns(small[SPAN + 16 : SPAN + 17, :], LANES)
-    shifted = (logs - jnp.log(delta)).T
+    shifted = ((logs - jnp.log(delta)) * LOG2E).T
     for k in range(CHUNKS):
         cols[k, :, 0:chunk_heads] = shifted[:, k * chunk_heads : (k + 1) * chunk_heads]
     ssq[...] = jnp.zeros_like(ssq)
@@ -246,9 +252,9 @@
             pad[j, 0:8, :] = halo_x[:, place].astype(jnp.float32)[HALO - 8 :]
             pad[j, 8 : 8 + SPAN, :] = x_buf[:, place].astype(jnp.float32)
             act = conv_silu(pad.at[j], cx_buf[:, place], taps)
-            turned = act.astype(jnp.float32).T
-            x_t[place, :] = turned.astype(jnp.bfloat16)
-            scaled = (turned * block_rows(mix_rows, k, j)).astype(jnp.bfloat16)
+            turned = act.T
+            x_t[place, :] = turned
+            scaled = (turned.astype(jnp.float32) * block_rows(mix_rows, k, j)).astype(jnp.bfloat16)
             upd[place, :] = jnp.dot(scaled, b_act[...], preferred_element_type=jnp.float32)
 
         @pl.when(early)
@@ -268,8 +274,7 @@
         shifts = cols[k]
         for j in range(blocks):
             place = block_place(k, j)
-            value = z_buf[:, place].astype(jnp.float32)
-            z_t[place, :] = (value / (1.0 + jnp.exp(-value))).T
+            z_t[place, :] = silu(z_buf[:, place].T.astype(jnp.float32))
             x_block = x_t[place, :]
             inner = []
             for i in range(per_block):
@@ -277,7 +282,7 @@
                 gap = (
                     log_rows[pl.ds(k * chunk_heads + which, 1), :] - shifts[:, which : which + 1]
                 )
-                weights = (scores[...] * jnp.exp(gap)).astype(jnp.bfloat16)
+                weights = (scores[...] * jnp.exp2(gap)).astype(jnp.bfloat16)
                 inner.append(
                     jnp.dot(
                         x_block[i * head : (i + 1) * head],
@@ -289,7 +294,7 @@
                 skip_rows, k, j
             ) * x_block.astype(jnp.float32)
 
-    ahead = jnp.where(early, 0, jnp.minimum(me - n // 2 + 1, CHUNKS))
+    ahead = jnp.where(early, 0, jnp.minimum(2 * (me - n // 2) + 2, CHUNKS))
 
     def within_ahead(k, carry):
         within(k)
@@ -297,10 +302,8 @@
 
     lax.fori_loop(0, ahead, within_ahead, 0)
 
-    def outputs(step, carry):
-        k = jnp.where(early, lax.rem(step + CHUNKS // 2, CHUNKS), step)
-
-        @pl.when(step >= ahead)
+    def outputs(k, carry):
+        @pl.when(k >= ahead)
         def _():
             within(k)
 

time: 62.3 us -> 53.1 us (0.85)
  Pallas kernels: 59.8 us -> 50.6 us
    pallas_call x1, Pallas kernels: 59.8 us -> 50.6 us  [shards(): pl.pallas_call(functools.partial(kernel, n), out_shape=jax.ShapeDtypeStru...]
where the time goes in v4:
time: 53.1 us; the launch traced here: 52.9 us
  Pallas kernels  50.6 us (95%)
  local copies, waits for them, and re-layouts  2.26 us (4%)
    pallas_call x1, Pallas kernels, shards(): pl.pallas_call(functools.partial(kernel, n), out_shape=jax.ShapeDtypeStru...  50.6 us
    unnamed x1, local copies, waits for them, and re-layouts  2.26 us

profile of v4, /device:TPU:0, one launch (start us, length us, event | category | flops | bytes accessed | tf_op | source)
XLA Modules:
  0.0 52.9 jit_solution(14550700027887481996)
XLA Ops:
  0.0 50.6 %shard_map.118 = bf16[512,1024]{1,0:T(8,128)(2,1)} custom-call(bf16[128,4096]{1,0:T(8,128)(2,1)} %x_ref.1, bf16[128,4096]{1,0:T(8,128)(2,1)} %z_ref.1, bf16[128,128]{1,0:T(8,128)(2,1)} %b_ref.1, bf16[128,128]{1,0:T(8,128)(2,1)} %c_ref.1, f32[64,128]{1,0:T(8,128)} %bitcast.5, f32[1,64]{1,0:T(1,128)} %bitcast.7, f32[1,64]{1,0:T(1,128)} %bitcast.8, ...), custom_call_target="tpu_custom_call" | custom-call | flops 536870912 | bytes 3145728 | tf_op jit(solution)/shard_map/pallas_call | solution.py:410
  50.6 2.3 %copy.14 = bf16[512,1024]{1,0:T(8,128)(2,1)} copy(bf16[512,1024]{1,0:T(8,128)(2,1)} %shard_map.118) | data formatting | bytes 2097152

commit v5 on v3

--- a/solution.py
+++ b/solution.py
@@ -74,6 +74,7 @@
     b_act,
     c_act,
     ssq,
+    above,
     load,
     halo_send,
     halo_recv,
@@ -99,14 +100,26 @@
 
     barrier = pltpu.get_barrier_semaphore()
 
-    def greet(other, carry):
-        @pl.when(other != me)
-        def _():
-            pl.semaphore_signal(barrier, inc=1, device_id={"ctx": other}, device_id_type=MESH)
-
-        return carry
-
-    lax.fori_loop(0, n, greet, 0)
+    def greet(other):
+        pl.semaphore_signal(barrier, inc=1, device_id={"ctx": other}, device_id_type=MESH)
+
+    @pl.when(me > 0)
+    def _():
+        greet(me - 1)
+
+    @pl.when(me < n - 1)
+    def _():
+        greet(me + 1)
+
+    def tell_above():
+        pl.semaphore_signal(above, inc=1, device_id={"ctx": me - 1}, device_id_type=MESH)
+
+    def pass_above():
+        pl.semaphore_wait(above, 1)
+
+        @pl.when(me > 0)
+        def _():
+            tell_above()
 
     def halo_copy(index):
         source = (x_ref, b_ref, c_ref)[index]
@@ -120,12 +133,15 @@
             device_id_type=MESH,
         )
 
-    def state_copy(k):
+    pieces = min(2, blocks)
+    piece = chunk // pieces
+
+    def state_copy(k, p):
         return pltpu.make_async_remote_copy(
-            src_ref=state_out.at[k],
-            dst_ref=state_in.at[k],
-            send_sem=state_send.at[k],
-            recv_sem=state_recv.at[k],
+            src_ref=state_out.at[k, pl.ds(p * piece, piece), :],
+            dst_ref=state_in.at[k, pl.ds(p * piece, piece), :],
+            send_sem=state_send.at[k, p],
+            recv_sem=state_recv.at[k, p],
             device_id={"ctx": nxt},
             device_id_type=MESH,
         )
@@ -194,7 +210,19 @@
         cols[k, :, 0:chunk_heads] = shifted[:, k * chunk_heads : (k + 1) * chunk_heads]
     ssq[...] = jnp.zeros_like(ssq)
 
-    pl.semaphore_wait(barrier, n - 1)
+    ends = (me == 0) | (me == n - 1)
+
+    @pl.when(ends)
+    def _():
+        pl.semaphore_wait(barrier, 1)
+
+    @pl.when(jnp.logical_not(ends))
+    def _():
+        pl.semaphore_wait(barrier, 2)
+
+    @pl.when(me == n - 1)
+    def _():
+        tell_above()
 
     @pl.when(me < n - 1)
     def _():
@@ -239,12 +267,20 @@
 
     early = me < n // 2
 
-    def forward(k):
-        for j in range(blocks):
-            entering = state_in[k, j * LANES : (j + 1) * LANES, :].astype(jnp.float32)
-            leaving = block_rows(last_rows, k, j) * entering + upd[block_place(k, j), :]
-            state_out[k, j * LANES : (j + 1) * LANES, :] = leaving.astype(jnp.bfloat16)
-        state_copy(k).start()
+    def chain(k):
+        for p in range(pieces):
+
+            @pl.when(me > 0)
+            def _():
+                state_copy(k, p).wait_recv()
+
+            @pl.when(me < n - 1)
+            def _():
+                for j in range(p * piece // LANES, (p + 1) * piece // LANES):
+                    entering = state_in[k, j * LANES : (j + 1) * LANES, :].astype(jnp.float32)
+                    leaving = block_rows(last_rows, k, j) * entering + upd[block_place(k, j), :]
+                    state_out[k, j * LANES : (j + 1) * LANES, :] = leaving.astype(jnp.bfloat16)
+                state_copy(k, p).start()
 
     def updates(k, carry):
         for j in range(blocks):
@@ -257,17 +293,26 @@
             scaled = (turned.astype(jnp.float32) * block_rows(mix_rows, k, j)).astype(jnp.bfloat16)
             upd[place, :] = jnp.dot(scaled, b_act[...], preferred_element_type=jnp.float32)
 
+        @pl.when(early & (me > 0) & (k == jnp.minimum(2 * (n // 2 - 1 - me), CHUNKS - 1)))
+        def _():
+            pass_above()
+
         @pl.when(early)
         def _():
-            @pl.when(me > 0)
-            def _():
-                state_copy(k).wait_recv()
-
-            forward(k)
+            chain(k)
 
         return carry
 
+    @pl.when(jnp.logical_not(early) & (me < n - 1))
+    def _():
+        pass_above()
+
     lax.fori_loop(0, CHUNKS, updates, 0)
+
+    @pl.when(me == 0)
+    def _():
+        pass_above()
+
     loading(6).wait()
 
     def within(k):
@@ -302,20 +347,14 @@
 
     lax.fori_loop(0, ahead, within_ahead, 0)
 
-    def outputs(step, carry):
-        k = jnp.where(early, lax.rem(step + CHUNKS // 2, CHUNKS), step)
-
-        @pl.when(step >= ahead)
+    def outputs(k, carry):
+        @pl.when(k >= ahead)
         def _():
             within(k)
 
         @pl.when(jnp.logical_not(early))
         def _():
-            state_copy(k).wait_recv()
-
-            @pl.when(me < n - 1)
-            def _():
-                forward(k)
+            chain(k)
 
         squares = ssq[0:1, :]
         for j in range(blocks):
@@ -380,7 +419,8 @@
             halo_copy(index).wait_send()
 
         def drain_state(k, carry):
-            state_copy(k).wait_send()
+            for p in range(pieces):
+                state_copy(k, p).wait_send()
             return carry
 
         lax.fori_loop(0, CHUNKS, drain_state, 0)
@@ -408,8 +448,9 @@
             own = gain_ref[pl.ds(me, 1), :]
         gain_col[...] = jnp.broadcast_to(own, (LANES, rows)).T
 
-    value = gated_ref[0].astype(jnp.float32) * scale_ref[0, 0:1, :] * gain_col[...]
-    out_ref[...] = value.astype(jnp.bfloat16)
+    for i in range(gated_ref.shape[0]):
+        value = gated_ref[i].astype(jnp.float32) * scale_ref[i, 0:1, :] * gain_col[...]
+        out_ref[:, i * SPAN : (i + 1) * SPAN] = value.astype(jnp.bfloat16)
 
 
 def shards(
@@ -466,11 +507,12 @@
             pltpu.VMEM((SPAN, state), bf16),
             pltpu.VMEM((SPAN, state), bf16),
             pltpu.VMEM((8, LANES), f32),
+            pltpu.SemaphoreType.REGULAR,
             dma((7,)),
             dma((3,)),
             dma((3,)),
-            dma((CHUNKS,)),
-            dma((CHUNKS,)),
+            dma((CHUNKS, 2)),
+            dma((CHUNKS, 2)),
             dma((n,)),
             dma((n,)),
             dma((n,)),
@@ -497,14 +539,14 @@
     )
     return pl.pallas_call(
         normalise,
-        grid=(n,),
+        grid=(2,),
         out_shape=jax.ShapeDtypeStruct((rows, n * SPAN), bf16),
         in_specs=[
-            pl.BlockSpec((1, rows, SPAN), lambda i: (i, 0, 0)),
-            pl.BlockSpec((1, 8, LANES), lambda i: (i, 0, 0)),
+            pl.BlockSpec((n // 2, rows, SPAN), lambda i: (i, 0, 0)),
+            pl.BlockSpec((n // 2, 8, LANES), lambda i: (i, 0, 0)),
             pl.BlockSpec(gain.shape, lambda i: (0, 0)),
         ],
-        out_specs=pl.BlockSpec((rows, SPAN), lambda i: (0, i)),
+        out_specs=pl.BlockSpec((rows, n // 2 * SPAN), lambda i: (0, i)),
         scratch_shapes=[pltpu.VMEM((rows, LANES), f32)],
         compiler_params=pltpu.CompilerParams(vmem_limit_bytes=56 * 1024 * 1024),
     )(gated, scales, gain)

time: 65.1 us -> 49.8 us (0.76)
  the two profiles are of different devices: /device:TPU:0 before, /device:TPU:19 now
where the time goes in v5:
time: 49.8 us; the launch traced here: 49.6 us
  Pallas kernels  49.6 us (100%)
    pallas_call x1, Pallas kernels, shards(): pl.pallas_call(functools.partial(kernel, n), out_shape=(jax.ShapeDtypeStr...  47.3 us
    pallas_call x1, Pallas kernels, shards(): pl.pallas_call(normalise, grid=(2,), out_shape=jax.ShapeDtypeStruct((rows...  2.31 us

profile of v5, /device:TPU:19, one launch (start us, length us, event | category | flops | bytes accessed | tf_op | source)
XLA Modules:
  0.0 49.6 jit_solution(12958331584048422763)
XLA Ops:
  0.0 47.3 %shard_map.118 = (bf16[8,512,128]{2,1,0:T(8,128)(2,1)}, f32[8,8,128]{2,1,0:T(8,128)}) custom-call(bf16[128,4096]{1,0:T(8,128)(2,1)} %x_ref.1, bf16[128,4096]{1,0:T(8,128)(2,1)} %z_ref.1, bf16[128,128]{1,0:T(8,128)(2,1)} %b_ref.1, bf16[128,128]{1,0:T(8,128)(2,1)} %c_ref.1, f32[64,128]{1,0:T(8,128)} %bitcast.5, f32[1,64]{1,0:T(1,128)} %bitcast.7, ...), custom_call_target="tpu_custom_call" | custom-call | flops 536870912 | bytes 3145728 | tf_op jit(solution)/shard_map/pallas_call | solution.py:471
  47.3 2.3 %shard_map.119 = bf16[512,1024]{1,0:T(8,128)(2,1)} custom-call(bf16[8,512,128]{2,1,0:T(8,128)(2,1)} %get-tuple-element.7.gated_ref, f32[8,8,128]{2,1,0:T(8,128)} %get-tuple-element.8.scale_ref, f32[1,4096]{1,0:T(1,128)} %bitcast.6), custom_call_target="tpu_custom_call" | custom-call | tf_op jit(solution)/shard_map/pallas_call | solution.py:540

commit v6 on v5

--- a/solution.py
+++ b/solution.py
@@ -70,6 +70,7 @@
     last_rows,
     skip_rows,
     cols,
+    turned_cols,
     scores,
     b_act,
     c_act,
@@ -122,13 +123,24 @@
             tell_above()
 
     def halo_copy(index):
-        source = (x_ref, b_ref, c_ref)[index]
-        target = (halo_x, halo_b, halo_c)[index]
+        source = (b_ref, c_ref)[index]
+        target = (halo_b, halo_c)[index]
         return pltpu.make_async_remote_copy(
             src_ref=source.at[pl.ds(SPAN - HALO, HALO), :],
             dst_ref=target,
-            send_sem=halo_send.at[index],
-            recv_sem=halo_recv.at[index],
+            send_sem=halo_send.at[CHUNKS + index],
+            recv_sem=halo_recv.at[CHUNKS + index],
+            device_id={"ctx": nxt},
+            device_id_type=MESH,
+        )
+
+    def halo_x_copy(k):
+        place = pl.ds(pl.multiple_of(k * chunk, LANES), chunk)
+        return pltpu.make_async_remote_copy(
+            src_ref=x_ref.at[pl.ds(SPAN - HALO, HALO), place],
+            dst_ref=halo_x.at[:, place],
+            send_sem=halo_send.at[k],
+            recv_sem=halo_recv.at[k],
             device_id={"ctx": nxt},
             device_id_type=MESH,
         )
@@ -201,14 +213,9 @@
     )
     last = jnp.broadcast_to(logs[:, SPAN - 1 : SPAN], (SPAN, LANES))
     log_rows[...] = logs * LOG2E
-    grow_rows[...] = jnp.exp(logs)
     mix_rows[...] = jnp.exp(last - logs) * delta
     last_rows[...] = jnp.exp(last)
-    skip_rows[...] = down_columns(small[SPAN + 16 : SPAN + 17, :], LANES)
-    shifted = ((logs - jnp.log(delta)) * LOG2E).T
-    for k in range(CHUNKS):
-        cols[k, :, 0:chunk_heads] = shifted[:, k * chunk_heads : (k + 1) * chunk_heads]
-    ssq[...] = jnp.zeros_like(ssq)
+    turned_cols[...] = (logs - jnp.log(delta)) * LOG2E
 
     ends = (me == 0) | (me == n - 1)
 
@@ -226,16 +233,23 @@
 
     @pl.when(me < n - 1)
     def _():
-        for index in range(3):
-            halo_copy(index).start()
+        halo_copy(0).start()
+        for k in range(CHUNKS):
+            halo_x_copy(k).start()
+        halo_copy(1).start()
+
+    early = me < n // 2
+
+    @pl.when(jnp.logical_not(early) & (me < n - 1))
+    def _():
+        pass_above()
 
     for index in range(6):
         loading(index).wait()
 
     @pl.when(me > 0)
     def _():
-        for index in range(3):
-            halo_copy(index).wait_recv()
+        halo_copy(0).wait_recv()
 
     @pl.when(me == 0)
     def _():
@@ -244,16 +258,12 @@
         halo_c[...] = jnp.zeros_like(halo_c)
         state_in[...] = jnp.zeros_like(state_in)
 
-    for index, (source, halo, weights, target) in enumerate(
-        ((b_buf, halo_b, cb_buf, b_act), (c_buf, halo_c, cc_buf, c_act))
-    ):
-        pad[index, 0:8, :] = halo[...].astype(jnp.float32)[HALO - 8 :]
-        pad[index, 8 : 8 + SPAN, :] = source[...].astype(jnp.float32)
-        target[...] = conv_silu(pad.at[index], weights[...], taps)
-    overlap = lax.dot_general(
-        b_act[...], c_act[...], (((1,), (1,)), ((), ())), preferred_element_type=jnp.float32
-    )
-    scores[...] = jnp.where(down <= across, overlap, 0.0)
+    def project(slot, source, halo, weights, target):
+        pad[slot, 0:8, :] = halo[...].astype(jnp.float32)[HALO - 8 :]
+        pad[slot, 8 : 8 + SPAN, :] = source[...].astype(jnp.float32)
+        target[...] = conv_silu(pad.at[slot], weights[...], taps)
+
+    project(0, b_buf, halo_b, cb_buf, b_act)
 
     def head_row(ref, index):
         return jnp.broadcast_to(ref[pl.ds(index, 1), :], (head, LANES))
@@ -264,8 +274,6 @@
 
     def block_place(k, j):
         return pl.ds(pl.multiple_of(k * chunk + j * LANES, LANES), LANES)
-
-    early = me < n // 2
 
     def chain(k):
         for p in range(pieces):
@@ -283,6 +291,10 @@
                 state_copy(k, p).start()
 
     def updates(k, carry):
+        @pl.when(me > 0)
+        def _():
+            halo_x_copy(k).wait_recv()
+
         for j in range(blocks):
             place = block_place(k, j)
             pad[j, 0:8, :] = halo_x[:, place].astype(jnp.float32)[HALO - 8 :]
@@ -293,7 +305,7 @@
             scaled = (turned.astype(jnp.float32) * block_rows(mix_rows, k, j)).astype(jnp.bfloat16)
             upd[place, :] = jnp.dot(scaled, b_act[...], preferred_element_type=jnp.float32)
 
-        @pl.when(early & (me > 0) & (k == jnp.minimum(2 * (n // 2 - 1 - me), CHUNKS - 1)))
+        @pl.when(early & (me > 0) & (k == jnp.minimum(2 * (n // 2 - 1 - me) + 1, CHUNKS - 1)))
         def _():
             pass_above()
 
@@ -303,16 +315,23 @@
 
         return carry
 
-    @pl.when(jnp.logical_not(early) & (me < n - 1))
-    def _():
-        pass_above()
-
     lax.fori_loop(0, CHUNKS, updates, 0)
 
-    @pl.when(me == 0)
-    def _():
-        pass_above()
-
+    @pl.when(me > 0)
+    def _():
+        halo_copy(1).wait_recv()
+
+    project(1, c_buf, halo_c, cc_buf, c_act)
+    overlap = lax.dot_general(
+        b_act[...], c_act[...], (((1,), (1,)), ((), ())), preferred_element_type=jnp.float32
+    )
+    scores[...] = jnp.where(down <= across, overlap, 0.0)
+    grow_rows[...] = jnp.exp2(log_rows[...])
+    skip_rows[...] = down_columns(small[SPAN + 16 : SPAN + 17, :], LANES)
+    shifted = turned_cols[...].T
+    for k in range(CHUNKS):
+        cols[k, :, 0:chunk_heads] = shifted[:, k * chunk_heads : (k + 1) * chunk_heads]
+    ssq[...] = jnp.zeros_like(ssq)
     loading(6).wait()
 
     def within(k):
@@ -340,12 +359,17 @@
             ) * x_block.astype(jnp.float32)
 
     ahead = jnp.where(early, 0, jnp.minimum(2 * (me - n // 2) + 2, CHUNKS))
+    ahead = jnp.where(me == 0, CHUNKS // 2, ahead)
 
     def within_ahead(k, carry):
         within(k)
         return carry
 
     lax.fori_loop(0, ahead, within_ahead, 0)
+
+    @pl.when(me == 0)
+    def _():
+        pass_above()
 
     def outputs(k, carry):
         @pl.when(k >= ahead)
@@ -415,10 +439,11 @@
 
     @pl.when(me < n - 1)
     def _():
-        for index in range(3):
+        for index in range(2):
             halo_copy(index).wait_send()
 
         def drain_state(k, carry):
+            halo_x_copy(k).wait_send()
             for p in range(pieces):
                 state_copy(k, p).wait_send()
             return carry
@@ -436,11 +461,12 @@
     lax.fori_loop(0, n, drain, 0)
 
 
-def normalise(gated_ref, scale_ref, gain_ref, out_ref, gain_col):
-    rows = out_ref.shape[0]
+def normalise(rows, gated_ref, scale_ref, gain_ref, out_ref, gain_col):
     me = lax.axis_index("ctx")
-
-    @pl.when(pl.program_id(0) == 0)
+    step = pl.program_id(0)
+    share = out_ref.shape[0]
+
+    @pl.when(step == 0)
     def _():
         if rows % LANES == 0:
             own = gain_ref[:, pl.ds(pl.multiple_of(me * rows, LANES), rows)]
@@ -448,8 +474,9 @@
             own = gain_ref[pl.ds(me, 1), :]
         gain_col[...] = jnp.broadcast_to(own, (LANES, rows)).T
 
+    gain = gain_col[pl.ds(pl.multiple_of(step * share, share), share), :]
     for i in range(gated_ref.shape[0]):
-        value = gated_ref[i].astype(jnp.float32) * scale_ref[i, 0:1, :] * gain_col[...]
+        value = gated_ref[i].astype(jnp.float32) * scale_ref[i, 0:1, :] * gain
         out_ref[:, i * SPAN : (i + 1) * SPAN] = value.astype(jnp.bfloat16)
 
 
@@ -504,13 +531,14 @@
             square,
             pltpu.VMEM((CHUNKS, SPAN, LANES), f32),
             square,
+            square,
             pltpu.VMEM((SPAN, state), bf16),
             pltpu.VMEM((SPAN, state), bf16),
             pltpu.VMEM((8, LANES), f32),
             pltpu.SemaphoreType.REGULAR,
             dma((7,)),
-            dma((3,)),
-            dma((3,)),
+            dma((CHUNKS + 2,)),
+            dma((CHUNKS + 2,)),
             dma((CHUNKS, 2)),
             dma((CHUNKS, 2)),
             dma((n,)),
@@ -537,16 +565,17 @@
         conv_b,
         conv_c,
     )
+    share = rows // 2 if rows % 256 == 0 else rows
     return pl.pallas_call(
-        normalise,
-        grid=(2,),
+        functools.partial(normalise, rows),
+        grid=(rows // share,),
         out_shape=jax.ShapeDtypeStruct((rows, n * SPAN), bf16),
         in_specs=[
-            pl.BlockSpec((n // 2, rows, SPAN), lambda i: (i, 0, 0)),
-            pl.BlockSpec((n // 2, 8, LANES), lambda i: (i, 0, 0)),
+            pl.BlockSpec((n, share, SPAN), lambda i: (0, i, 0)),
+            pl.BlockSpec((n, 8, LANES), lambda i: (0, 0, 0)),
             pl.BlockSpec(gain.shape, lambda i: (0, 0)),
         ],
-        out_specs=pl.BlockSpec((rows, n // 2 * SPAN), lambda i: (0, i)),
+        out_specs=pl.BlockSpec((share, n * SPAN), lambda i: (i, 0)),
         scratch_shapes=[pltpu.VMEM((rows, LANES), f32)],
         compiler_params=pltpu.CompilerParams(vmem_limit_bytes=56 * 1024 * 1024),
     )(gated, scales, gain)

time: 49.8 us -> 49.7 us (level)
  no operation moved by 1% of the time
where the time goes in v6:
time: 49.7 us; the launch traced here: 49.5 us
  Pallas kernels  49.5 us (100%)
    pallas_call x1, Pallas kernels, shards(): pl.pallas_call(functools.partial(kernel, n), out_shape=(jax.ShapeDtypeStr...  47.1 us
    pallas_call x1, Pallas kernels, shards(): pl.pallas_call(functools.partial(normalise, rows), grid=(rows // share,),...  2.36 us

profile of v6, /device:TPU:19, one launch (start us, length us, event | category | flops | bytes accessed | tf_op | source)
XLA Modules:
  0.0 49.5 jit_solution(6546774904005147807)
XLA Ops:
  0.0 47.1 %shard_map.118 = (bf16[8,512,128]{2,1,0:T(8,128)(2,1)}, f32[8,8,128]{2,1,0:T(8,128)}) custom-call(bf16[128,4096]{1,0:T(8,128)(2,1)} %x_ref.1, bf16[128,4096]{1,0:T(8,128)(2,1)} %z_ref.1, bf16[128,128]{1,0:T(8,128)(2,1)} %b_ref.1, bf16[128,128]{1,0:T(8,128)(2,1)} %c_ref.1, f32[64,128]{1,0:T(8,128)} %bitcast.5, f32[1,64]{1,0:T(1,128)} %bitcast.7, ...), custom_call_target="tpu_custom_call" | custom-call | flops 536870912 | bytes 3145728 | tf_op jit(solution)/shard_map/pallas_call | solution.py:498
  47.1 2.4 %shard_map.119 = bf16[512,1024]{1,0:T(8,128)(2,1)} custom-call(bf16[8,512,128]{2,1,0:T(8,128)(2,1)} %get-tuple-element.7.gated_ref, f32[8,8,128]{2,1,0:T(8,128)} %get-tuple-element.8.scale_ref, f32[1,4096]{1,0:T(1,128)} %bitcast.6), custom_call_target="tpu_custom_call" | custom-call | tf_op jit(solution)/shard_map/pallas_call | solution.py:569

commit v7 on v6

--- a/solution.py
+++ b/solution.py
@@ -234,9 +234,10 @@
     @pl.when(me < n - 1)
     def _():
         halo_copy(0).start()
-        for k in range(CHUNKS):
+        halo_x_copy(0).start()
+        halo_copy(1).start()
+        for k in range(1, CHUNKS):
             halo_x_copy(k).start()
-        halo_copy(1).start()
 
     early = me < n // 2
 
@@ -290,49 +291,22 @@
                     state_out[k, j * LANES : (j + 1) * LANES, :] = leaving.astype(jnp.bfloat16)
                 state_copy(k, p).start()
 
-    def updates(k, carry):
+    def set_up():
         @pl.when(me > 0)
         def _():
-            halo_x_copy(k).wait_recv()
-
-        for j in range(blocks):
-            place = block_place(k, j)
-            pad[j, 0:8, :] = halo_x[:, place].astype(jnp.float32)[HALO - 8 :]
-            pad[j, 8 : 8 + SPAN, :] = x_buf[:, place].astype(jnp.float32)
-            act = conv_silu(pad.at[j], cx_buf[:, place], taps)
-            turned = act.T
-            x_t[place, :] = turned
-            scaled = (turned.astype(jnp.float32) * block_rows(mix_rows, k, j)).astype(jnp.bfloat16)
-            upd[place, :] = jnp.dot(scaled, b_act[...], preferred_element_type=jnp.float32)
-
-        @pl.when(early & (me > 0) & (k == jnp.minimum(2 * (n // 2 - 1 - me) + 1, CHUNKS - 1)))
-        def _():
-            pass_above()
-
-        @pl.when(early)
-        def _():
-            chain(k)
-
-        return carry
-
-    lax.fori_loop(0, CHUNKS, updates, 0)
-
-    @pl.when(me > 0)
-    def _():
-        halo_copy(1).wait_recv()
-
-    project(1, c_buf, halo_c, cc_buf, c_act)
-    overlap = lax.dot_general(
-        b_act[...], c_act[...], (((1,), (1,)), ((), ())), preferred_element_type=jnp.float32
-    )
-    scores[...] = jnp.where(down <= across, overlap, 0.0)
-    grow_rows[...] = jnp.exp2(log_rows[...])
-    skip_rows[...] = down_columns(small[SPAN + 16 : SPAN + 17, :], LANES)
-    shifted = turned_cols[...].T
-    for k in range(CHUNKS):
-        cols[k, :, 0:chunk_heads] = shifted[:, k * chunk_heads : (k + 1) * chunk_heads]
-    ssq[...] = jnp.zeros_like(ssq)
-    loading(6).wait()
+            halo_copy(1).wait_recv()
+
+        project(1, c_buf, halo_c, cc_buf, c_act)
+        overlap = lax.dot_general(
+            b_act[...], c_act[...], (((1,), (1,)), ((), ())), preferred_element_type=jnp.float32
+        )
+        scores[...] = jnp.where(down <= across, overlap, 0.0)
+        grow_rows[...] = jnp.exp2(log_rows[...])
+        skip_rows[...] = down_columns(small[SPAN + 16 : SPAN + 17, :], LANES)
+        shifted = turned_cols[...].T
+        for k in range(CHUNKS):
+            cols[k, :, 0:chunk_heads] = shifted[:, k * chunk_heads : (k + 1) * chunk_heads]
+        ssq[...] = jnp.zeros_like(ssq)
 
     def within(k):
         shifts = cols[k]
@@ -358,21 +332,76 @@
                 skip_rows, k, j
             ) * x_block.astype(jnp.float32)
 
-    ahead = jnp.where(early, 0, jnp.minimum(2 * (me - n // 2) + 2, CHUNKS))
+    far_first = early & (me > 0)
+    lag = jnp.where(far_first, jnp.minimum(2 * (me - 1), CHUNKS), 0)
+
+    def order(step):
+        return jnp.where(far_first, lax.rem(step + CHUNKS // 2, CHUNKS), step)
+
+    def updates(k):
+        @pl.when(me > 0)
+        def _():
+            halo_x_copy(k).wait_recv()
+
+        for j in range(blocks):
+            place = block_place(k, j)
+            pad[j, 0:8, :] = halo_x[:, place].astype(jnp.float32)[HALO - 8 :]
+            pad[j, 8 : 8 + SPAN, :] = x_buf[:, place].astype(jnp.float32)
+            act = conv_silu(pad.at[j], cx_buf[:, place], taps)
+            turned = act.T
+            x_t[place, :] = turned
+            scaled = (turned.astype(jnp.float32) * block_rows(mix_rows, k, j)).astype(jnp.bfloat16)
+            upd[place, :] = jnp.dot(scaled, b_act[...], preferred_element_type=jnp.float32)
+
+    def advance(step, carry):
+        @pl.when(step < CHUNKS)
+        def _():
+            updates(step)
+
+        @pl.when(step >= CHUNKS)
+        def _():
+            within(order(step - CHUNKS))
+
+        turn = lag + jnp.minimum(2 * (n // 2 - 1 - me) + 1, CHUNKS - 1)
+
+        @pl.when(far_first & (step == turn))
+        def _():
+            pass_above()
+
+        @pl.when(early & (step >= lag))
+        def _():
+            chain(step - lag)
+
+        return carry
+
+    @pl.when(me > 1)
+    def _():
+        set_up()
+
+    loading(6).wait()
+    lax.fori_loop(0, CHUNKS + lag, advance, 0)
+
+    @pl.when(me <= 1)
+    def _():
+        set_up()
+
+    ahead = jnp.where(early, lag, jnp.minimum(2 * (me - n // 2) + 2, CHUNKS))
     ahead = jnp.where(me == 0, CHUNKS // 2, ahead)
 
     def within_ahead(k, carry):
         within(k)
         return carry
 
-    lax.fori_loop(0, ahead, within_ahead, 0)
+    lax.fori_loop(lag, ahead, within_ahead, 0)
 
     @pl.when(me == 0)
     def _():
         pass_above()
 
-    def outputs(k, carry):
-        @pl.when(k >= ahead)
+    def outputs(step, carry):
+        k = order(step)
+
+        @pl.when(step >= ahead)
         def _():
             within(k)
 

time: 49.7 us -> 57.9 us (1.16)
  the two profiles are of different devices: /device:TPU:19 before, /device:TPU:0 now
where the time goes in v7:
time: 57.9 us; the launch traced here: 57.7 us
  Pallas kernels  57.7 us (100%)
    pallas_call x1, Pallas kernels, shards(): pl.pallas_call(functools.partial(kernel, n), out_shape=(jax.ShapeDtypeStr...  55.4 us
    pallas_call x1, Pallas kernels, shards(): pl.pallas_call(functools.partial(normalise, rows), grid=(rows // share,),...  2.36 us

profile of v7, /device:TPU:0, one launch (start us, length us, event | category | flops | bytes accessed | tf_op | source)
XLA Modules:
  0.0 57.7 jit_solution(5615258546329711666)
XLA Ops:
  0.0 55.4 %shard_map.118 = (bf16[8,512,128]{2,1,0:T(8,128)(2,1)}, f32[8,8,128]{2,1,0:T(8,128)}) custom-call(bf16[128,4096]{1,0:T(8,128)(2,1)} %x_ref.1, bf16[128,4096]{1,0:T(8,128)(2,1)} %z_ref.1, bf16[128,128]{1,0:T(8,128)(2,1)} %b_ref.1, bf16[128,128]{1,0:T(8,128)(2,1)} %c_ref.1, f32[64,128]{1,0:T(8,128)} %bitcast.5, f32[1,64]{1,0:T(1,128)} %bitcast.7, ...), custom_call_target="tpu_custom_call" | custom-call | flops 536870912 | bytes 3145728 | tf_op jit(solution)/shard_map/pallas_call | solution.py:527
  55.4 2.4 %shard_map.119 = bf16[512,1024]{1,0:T(8,128)(2,1)} custom-call(bf16[8,512,128]{2,1,0:T(8,128)(2,1)} %get-tuple-element.7.gated_ref, f32[8,8,128]{2,1,0:T(8,128)} %get-tuple-element.8.scale_ref, f32[1,4096]{1,0:T(1,128)} %bitcast.6), custom_call_target="tpu_custom_call" | custom-call | tf_op jit(solution)/shard_map/pallas_call | solution.py:598

commit v8 on v7

--- a/solution.py
+++ b/solution.py
@@ -332,11 +332,8 @@
                 skip_rows, k, j
             ) * x_block.astype(jnp.float32)
 
-    far_first = early & (me > 0)
-    lag = jnp.where(far_first, jnp.minimum(2 * (me - 1), CHUNKS), 0)
-
-    def order(step):
-        return jnp.where(far_first, lax.rem(step + CHUNKS // 2, CHUNKS), step)
+    middle = early & (me > 0)
+    lag = jnp.where(middle, jnp.minimum(2 * (me - 1), CHUNKS), 0)
 
     def updates(k):
         @pl.when(me > 0)
@@ -360,11 +357,11 @@
 
         @pl.when(step >= CHUNKS)
         def _():
-            within(order(step - CHUNKS))
+            within(step - CHUNKS)
 
         turn = lag + jnp.minimum(2 * (n // 2 - 1 - me) + 1, CHUNKS - 1)
 
-        @pl.when(far_first & (step == turn))
+        @pl.when(middle & (step == turn))
         def _():
             pass_above()
 
@@ -398,10 +395,8 @@
     def _():
         pass_above()
 
-    def outputs(step, carry):
-        k = order(step)
-
-        @pl.when(step >= ahead)
+    def outputs(k, carry):
+        @pl.when(k >= ahead)
         def _():
             within(k)
 

time: 57.9 us -> 49.1 us (0.85)
  the two profiles are of different devices: /device:TPU:0 before, /device:TPU:23 now
where the time goes in v8:
time: 49.1 us; the launch traced here: 48.8 us
  Pallas kernels  48.8 us (99%)
    pallas_call x1, Pallas kernels, shards(): pl.pallas_call(functools.partial(kernel, n), out_shape=(jax.ShapeDtypeStr...  46.5 us
    pallas_call x1, Pallas kernels, shards(): pl.pallas_call(functools.partial(normalise, rows), grid=(rows // share,),...  2.36 us

profile of v8, /device:TPU:23, one launch (start us, length us, event | category | flops | bytes accessed | tf_op | source)
XLA Modules:
  0.0 48.8 jit_solution(7703108831976517330)
XLA Ops:
  0.0 46.5 %shard_map.118 = (bf16[8,512,128]{2,1,0:T(8,128)(2,1)}, f32[8,8,128]{2,1,0:T(8,128)}) custom-call(bf16[128,4096]{1,0:T(8,128)(2,1)} %x_ref.1, bf16[128,4096]{1,0:T(8,128)(2,1)} %z_ref.1, bf16[128,128]{1,0:T(8,128)(2,1)} %b_ref.1, bf16[128,128]{1,0:T(8,128)(2,1)} %c_ref.1, f32[64,128]{1,0:T(8,128)} %bitcast.5, f32[1,64]{1,0:T(1,128)} %bitcast.7, ...), custom_call_target="tpu_custom_call" | custom-call | flops 536870912 | bytes 3145728 | tf_op jit(solution)/shard_map/pallas_call | solution.py:522
  46.5 2.4 %shard_map.119 = bf16[512,1024]{1,0:T(8,128)(2,1)} custom-call(bf16[8,512,128]{2,1,0:T(8,128)(2,1)} %get-tuple-element.7.gated_ref, f32[8,8,128]{2,1,0:T(8,128)} %get-tuple-element.8.scale_ref, f32[1,4096]{1,0:T(1,128)} %bitcast.6), custom_call_target="tpu_custom_call" | custom-call | tf_op jit(solution)/shard_map/pallas_call | solution.py:593

commit v9 on v7

--- a/solution.py
+++ b/solution.py
@@ -332,8 +332,10 @@
                 skip_rows, k, j
             ) * x_block.astype(jnp.float32)
 
-    far_first = early & (me > 0)
-    lag = jnp.where(far_first, jnp.minimum(2 * (me - 1), CHUNKS), 0)
+    middle = early & (me > 0)
+    lag = jnp.where(middle, jnp.minimum(2 * (me - 1), CHUNKS), 0)
+
+    far_first = me == n // 2 - 1
 
     def order(step):
         return jnp.where(far_first, lax.rem(step + CHUNKS // 2, CHUNKS), step)
@@ -364,7 +366,7 @@
 
         turn = lag + jnp.minimum(2 * (n // 2 - 1 - me) + 1, CHUNKS - 1)
 
-        @pl.when(far_first & (step == turn))
+        @pl.when(middle & (step == turn))
         def _():
             pass_above()
 

time: 57.9 us -> 49 us (0.85)
  the two profiles are of different devices: /device:TPU:0 before, /device:TPU:17 now
where the time goes in v9:
time: 49 us; the launch traced here: 48.8 us
  Pallas kernels  48.8 us (100%)
    pallas_call x1, Pallas kernels, shards(): pl.pallas_call(functools.partial(kernel, n), out_shape=(jax.ShapeDtypeStr...  46.4 us
    pallas_call x1, Pallas kernels, shards(): pl.pallas_call(functools.partial(normalise, rows), grid=(rows // share,),...  2.36 us

profile of v9, /device:TPU:17, one launch (start us, length us, event | category | flops | bytes accessed | tf_op | source)
XLA Modules:
  0.0 48.8 jit_solution(12462580530888980012)
XLA Ops:
  0.0 46.4 %shard_map.118 = (bf16[8,512,128]{2,1,0:T(8,128)(2,1)}, f32[8,8,128]{2,1,0:T(8,128)}) custom-call(bf16[128,4096]{1,0:T(8,128)(2,1)} %x_ref.1, bf16[128,4096]{1,0:T(8,128)(2,1)} %z_ref.1, bf16[128,128]{1,0:T(8,128)(2,1)} %b_ref.1, bf16[128,128]{1,0:T(8,128)(2,1)} %c_ref.1, f32[64,128]{1,0:T(8,128)} %bitcast.5, f32[1,64]{1,0:T(1,128)} %bitcast.7, ...), custom_call_target="tpu_custom_call" | custom-call | flops 536870912 | bytes 3145728 | tf_op jit(solution)/shard_map/pallas_call | solution.py:529
  46.4 2.4 %shard_map.119 = bf16[512,1024]{1,0:T(8,128)(2,1)} custom-call(bf16[8,512,128]{2,1,0:T(8,128)(2,1)} %get-tuple-element.7.gated_ref, f32[8,8,128]{2,1,0:T(8,128)} %get-tuple-element.8.scale_ref, f32[1,4096]{1,0:T(1,128)} %bitcast.6), custom_call_target="tpu_custom_call" | custom-call | tf_op jit(solution)/shard_map/pallas_call | solution.py:600

commit v10 on v9

--- a/solution.py
+++ b/solution.py
@@ -145,7 +145,7 @@
             device_id_type=MESH,
         )
 
-    pieces = min(2, blocks)
+    pieces = min(4, blocks)
     piece = chunk // pieces
 
     def state_copy(k, p):
@@ -570,8 +570,8 @@
             dma((7,)),
             dma((CHUNKS + 2,)),
             dma((CHUNKS + 2,)),
-            dma((CHUNKS, 2)),
-            dma((CHUNKS, 2)),
+            dma((CHUNKS, 4)),
+            dma((CHUNKS, 4)),
             dma((n,)),
             dma((n,)),
             dma((n,)),

time: 49 us -> 48.9 us (level)
  no operation moved by 1% of the time
where the time goes in v10:
time: 48.9 us; the launch traced here: 48.7 us
  Pallas kernels  48.7 us (100%)
    pallas_call x1, Pallas kernels, shards(): pl.pallas_call(functools.partial(kernel, n), out_shape=(jax.ShapeDtypeStr...  46.3 us
    pallas_call x1, Pallas kernels, shards(): pl.pallas_call(functools.partial(normalise, rows), grid=(rows // share,),...  2.36 us

profile of v10, /device:TPU:17, one launch (start us, length us, event | category | flops | bytes accessed | tf_op | source)
XLA Modules:
  0.0 48.7 jit_solution(13030514024991240238)
XLA Ops:
  0.0 46.3 %shard_map.118 = (bf16[8,512,128]{2,1,0:T(8,128)(2,1)}, f32[8,8,128]{2,1,0:T(8,128)}) custom-call(bf16[128,4096]{1,0:T(8,128)(2,1)} %x_ref.1, bf16[128,4096]{1,0:T(8,128)(2,1)} %z_ref.1, bf16[128,128]{1,0:T(8,128)(2,1)} %b_ref.1, bf16[128,128]{1,0:T(8,128)(2,1)} %c_ref.1, f32[64,128]{1,0:T(8,128)} %bitcast.5, f32[1,64]{1,0:T(1,128)} %bitcast.7, ...), custom_call_target="tpu_custom_call" | custom-call | flops 536870912 | bytes 3145728 | tf_op jit(solution)/shard_map/pallas_call | solution.py:529
  46.3 2.4 %shard_map.119 = bf16[512,1024]{1,0:T(8,128)(2,1)} custom-call(bf16[8,512,128]{2,1,0:T(8,128)(2,1)} %get-tuple-element.7.gated_ref, f32[8,8,128]{2,1,0:T(8,128)} %get-tuple-element.8.scale_ref, f32[1,4096]{1,0:T(1,128)} %bitcast.6), custom_call_target="tpu_custom_call" | custom-call | tf_op jit(solution)/shard_map/pallas_call | solution.py:600
